TPU v7x, 256 devices: a whole 4x4x8 slice. The times are simulated.
256 devices in a mesh: morton: 128 (over z, x, y), dp: 2 (over core).
Axes of the slice: x: 4, y: 4, z: 8, core: 2. Of those that a mesh axis runs over, the one named last changes fastest.
Arguments:
- node_feat: bfloat16 [2, 65536, 128], P('dp', 'morton'), may hold values from -6 to 6
- edge_feat: bfloat16 [2, 262144, 128], P('dp', 'morton'), may hold values from -6 to 6
- cot_node: bfloat16 [2, 65536, 128], P('dp', 'morton'), may hold values from -6 to 6
- cot_edge: bfloat16 [2, 262144, 128], P('dp', 'morton'), may hold values from -6 to 6
- senders: int32 [2, 262144], P('dp', 'morton'), may hold values from 0 to 767, as said below
- receivers: int32 [2, 262144], P('dp', 'morton'), may hold values from 0 to 511
- send_rows: int32 [2, 32768], P('dp', 'morton'), may hold values from 0 to 511
- edge_count: int32 [2, 128], P('dp', 'morton'), may hold values from 512 to 2048, as said below
- edge_w1: float32 [384, 128], replicated, may hold values from -0.3125 to 0.3125
- edge_w2: float32 [128, 128], replicated, may hold values from -0.5 to 0.5
- edge_gain: float32 [128], replicated, may hold values from 0.25 to 1.75
- node_w1: float32 [256, 128], replicated, may hold values from -0.375 to 0.375
- node_w2: float32 [128, 128], replicated, may hold values from -0.5 to 0.5
- node_gain: float32 [128], replicated, may hold values from 0.25 to 1.75
Outputs:
- grad_node: float32 [2, 65536, 128], P('dp', 'morton')
- grad_edge: float32 [2, 262144, 128], P('dp', 'morton')
- grad_edge_w1: float32 [384, 128], replicated
- grad_edge_w2: float32 [128, 128], replicated
- grad_edge_gain: float32 [128], replicated
- grad_node_w1: float32 [256, 128], replicated
- grad_node_w2: float32 [128, 128], replicated
- grad_node_gain: float32 [128], replicated
Inputs may be any that keep to these rules, and one draw needn't show every extreme that they name: `senders`: on device m, an entry below 512 is one of its own cells; an entry 512 + k * 64 + q is ghost row q of group k, which comes from device m - d_k with d = (-128/2, -1, +1, +128/2); that device always exists. `send_rows`: entry k * 64 + q of device m is its local cell sent to device m + d_k, with d = (-128/2, -1, +1, +128/2). `edge_count`: edge slots at or beyond the count are empty; some device of every block is full.
All inputs are finite; a program needn't handle non-finite values.
Results may differ from a plain program's by a relative error of at most 0.014.
Values may be sent and summed in bfloat16 or wider, within the bound.
A program may use at most 64 MiB of HBM per device.

v0:
```python
import jax
import jax.numpy as jnp
from jax import lax
from jax.sharding import Mesh
from jax.sharding import PartitionSpec as P

MORTON = ("morton_0", "morton_1", "morton_2")


def from_behind(value, axis, by):
    devices = lax.axis_size(axis)
    pairs = [(i, i + by) for i in range(devices) if 0 <= i + by < devices]
    return lax.ppermute(value, axis, pairs)


def cut_along(value, dim, devices):
    lengths = value.shape
    tiles = value.reshape(*lengths[:dim], devices, lengths[dim] // devices, *lengths[dim + 1 :])
    return jnp.moveaxis(tiles, dim, 0)


def sent_and_summed(value, axis, dim):
    devices = lax.axis_size(axis)
    tiles = lax.all_to_all(cut_along(value, dim, devices), axis, 0, 0, tiled=True)
    return jnp.sum(tiles, axis=0)


def sum_in_two_steps(value, axes, dim):
    far, near = axes
    own = sent_and_summed(cut_along(value, dim, lax.axis_size(far)), near, dim + 1)
    return jnp.sum(lax.all_to_all(own, far, 0, 0, tiled=True), axis=0)


def padded_to(lines, devices):
    spare = -len(lines) % devices
    return jnp.pad(lines, [(0, spare)] + [(0, 0)] * (lines.ndim - 1))


def from_everyone(value, axis):
    devices = lax.axis_size(axis)
    return lax.all_to_all(
        jnp.broadcast_to(value[None], (devices, *value.shape)), axis, 0, 0, tiled=True
    )


def joined_along(tiles, dim):
    tiles = jnp.moveaxis(tiles, 0, dim)
    lengths = tiles.shape
    return tiles.reshape(*lengths[:dim], lengths[dim] * lengths[dim + 1], *lengths[dim + 2 :])


def whole_of(value, axes, dim):
    far, near = axes
    tiles = from_everyone(from_everyone(value, far), near)
    return joined_along(tiles.swapaxes(0, 1).reshape(-1, *value.shape), dim)


def total_of(value, axes):
    own = sum_in_two_steps(
        padded_to(value, lax.axis_size(axes[0]) * lax.axis_size(axes[1])), axes, 0
    )
    whole = whole_of(own, axes, 0)
    return whole[: len(value)].reshape(value.shape)


def together(arrays, axis):
    ends = [0]
    for a in arrays:
        ends.append(ends[-1] + a.size)
    subtotal = total_of(jnp.concatenate([a.ravel() for a in arrays]), axis)
    return tuple((subtotal[b:e].reshape(a.shape) for a, b, e in zip(arrays, ends, ends[1:])))


def layer_norm(values, gain):
    center = values - jnp.mean(values, axis=-1, keepdims=True)
    spread = jnp.mean(center * center, axis=-1, keepdims=True)
    return center * lax.rsqrt(spread + 1e-05) * gain


def local_forward(
    cells, ghosts, edges, ew1, ew2, egain, nw1, nw2, ngain, sending, receiving, count
):
    table = jnp.concatenate([cells, ghosts], axis=0)
    joined = jnp.concatenate(
        [
            edges.astype(jnp.bfloat16),
            table[sending].astype(jnp.bfloat16),
            cells[receiving].astype(jnp.bfloat16),
        ],
        axis=1,
    )
    first = jnp.dot(joined, ew1.astype(jnp.bfloat16), preferred_element_type=jnp.float32)
    second = jnp.dot(
        jax.nn.silu(first).astype(jnp.bfloat16),
        ew2.astype(jnp.bfloat16),
        preferred_element_type=jnp.float32,
    )
    live = (jnp.arange(edges.shape[0]) < count).astype(edges.dtype)[:, None]
    edge_new = edges + live * layer_norm(second, egain)
    message = (live * edge_new).astype(jnp.bfloat16)
    gathered = jax.ops.segment_sum(
        message.astype(edges.dtype), receiving, num_segments=cells.shape[0]
    )
    stacked = jnp.concatenate([cells.astype(jnp.bfloat16), gathered.astype(jnp.bfloat16)], axis=1)
    hidden = jnp.dot(stacked, nw1.astype(jnp.bfloat16), preferred_element_type=jnp.float32)
    output = jnp.dot(
        jax.nn.silu(hidden).astype(jnp.bfloat16),
        nw2.astype(jnp.bfloat16),
        preferred_element_type=jnp.float32,
    )
    return (cells + layer_norm(output, ngain), edge_new)


def on_device(
    node_feat,
    edge_feat,
    cot_node,
    cot_edge,
    senders,
    receivers,
    send_rows,
    edge_count,
    edge_w1,
    edge_w2,
    edge_gain,
    node_w1,
    node_w2,
    node_gain,
):
    peers = lax.axis_size(MORTON)
    offsets = (-(peers // 2), -1, 1, peers // 2)
    width = node_feat.shape[2]
    quota = send_rows.shape[1] // 4
    outgoing = send_rows[0].reshape(4, quota)
    cells_bf = node_feat[0]
    picked = [cells_bf[outgoing[k]] for k in range(4)]
    arrived = []
    for k in range(4):
        moved = from_behind(picked[k], MORTON, offsets[k])
        arrived.append(moved.astype(jnp.float32))
    ghosts = jnp.concatenate(arrived, axis=0)
    cells = cells_bf.astype(jnp.float32)
    edges = edge_feat[0].astype(jnp.float32)
    sending = senders[0]
    receiving = receivers[0]
    count = edge_count[0, 0]

    def forward(cells, ghosts, edges, ew1, ew2, egain, nw1, nw2, ngain):
        return local_forward(
            cells, ghosts, edges, ew1, ew2, egain, nw1, nw2, ngain, sending, receiving, count
        )

    outputs, pullback = jax.vjp(
        forward, cells, ghosts, edges, edge_w1, edge_w2, edge_gain, node_w1, node_w2, node_gain
    )
    grads = pullback((cot_node[0].astype(jnp.float32), cot_edge[0].astype(jnp.float32)))
    grad_cells = grads[0]
    ghost_grads = grads[1].reshape(4, quota, width)
    for k in range(4):
        back = from_behind(ghost_grads[k].astype(jnp.bfloat16), MORTON, -offsets[k]).astype(
            jnp.float32
        )
        grad_cells = grad_cells.at[outgoing[k]].add(back)
    summed = together(
        (grads[3], grads[4], grads[5], grads[6], grads[7], grads[8]),
        (("morton_0", "morton_1"), ("morton_2", "dp")),
    )
    factor = 1.0 / jnp.sqrt(jnp.float32(lax.axis_size("dp") * peers * edge_feat.shape[1]))
    return (
        grad_cells[None],
        grads[2][None],
        summed[0] * factor,
        summed[1] * factor,
        summed[2] * factor,
        summed[3] * factor,
        summed[4] * factor,
        summed[5] * factor,
    )


def solution(mesh):
    split = Mesh(
        mesh.devices.reshape(8, 4, 4, mesh.shape["dp"]), ("morton_0", "morton_1", "morton_2", "dp")
    )
    return jax.shard_map(
        on_device,
        mesh=split,
        in_specs=(
            P("dp", MORTON, None),
            P("dp", MORTON, None),
            P("dp", MORTON, None),
            P("dp", MORTON, None),
            P("dp", MORTON),
            P("dp", MORTON),
            P("dp", MORTON),
            P("dp", MORTON),
            P(),
            P(),
            P(),
            P(),
            P(),
            P(),
        ),
        out_specs=(P("dp", MORTON, None), P("dp", MORTON, None), P(), P(), P(), P(), P(), P()),
        check_vma=False,
    )
```

profile of v0, /device:TPU:1, one launch (start us, length us, event | category | flops | bytes accessed | tf_op | source)
XLA Modules:
  0.0 183.1 jit_solution(17777540278140829023)
XLA Ops:
  0.7 0.9 fusion.61
  1.6 1.5 gather_fusion.3
  3.1 9.6 %collective-permute-start.3 = (bf16[64,128]{1,0:T(8,128)(2,1)S(1)}, bf16[64,128]{1,0:T(8,128)(2,1)S(1)}, u32[]{:S(2)}, u32[]{:S(2)}) collective-permute-start(bf16[64,128]{1,0:T(8,128)(2,1)S(1)} %gather_fusion.3), channel_id=1, source_target_pairs={{0,128},{2,130},{4,132},{6,134},{8,136},{10,138},{12,140},{14,142}... | collective-permute-start | bytes 49160 | tf_op jit(solution)/shard_map/ppermute | solution.py:13
  12.7 1.5 gather_fusion.1
  14.3 1.3 collective-permute-start.1
  15.6 1.6 gather_fusion
  17.2 1.3 collective-permute-start
  18.5 1.5 gather_fusion.2
  20.0 4.0 %collective-permute-start.2 = (bf16[64,128]{1,0:T(8,128)(2,1)S(1)}, bf16[64,128]{1,0:T(8,128)(2,1)S(1)}, u32[]{:S(2)}, u32[]{:S(2)}) collective-permute-start(bf16[64,128]{1,0:T(8,128)(2,1)S(1)} %gather_fusion.2), channel_id=1, source_target_pairs={{0,2},{2,4},{4,6},{6,8},{8,10},{10,12},{12,14},{14,16},{16,18},{18... | collective-permute-start | bytes 49160 | tf_op jit(solution)/shard_map/ppermute | solution.py:13
  24.0 0.7 and_reduce_fusion
  24.7 0.7 compare_select_fusion
  25.5 0.9 convert_dynamic-update-slice_fusion
  27.0 0.7 compare_select_fusion.1
  27.8 0.7 broadcast_clamp_fusion
  28.5 1.0 copy.63
  30.0 6.2 %gather_fusion.5 = bf16[2048,128]{1,0:T(8,128)(2,1)S(1)} fusion(bf16[512,128]{1,0:T(8,128)(2,1)S(1)} %bitcast.93, s32[2048]{0:T(1024)S(1)} %get-tuple-element.70), kind=kCustom, calls=%fused_computation.5 | custom fusion | bytes 1056768 | tf_op jit(solution)/shard_map/jvp()/gather | solution.py:88
  36.5 6.2 %gather_fusion.4 = bf16[2048,128]{1,0:T(8,128)(2,1)S(1)} fusion(bf16[768,128]{1,0:T(8,128)(2,1)S(1)} %convert_dynamic-update-slice_fusion.1, s32[2048]{0:T(1024)S(1)} %broadcast_clamp_fusion.2), kind=kCustom, calls=%fused_computation.4 | custom fusion | bytes 1056768 | tf_op jit(solution)/shard_map/jvp()/gather | solution.py:87
  43.0 0.6 fusion.17
  43.9 0.5 fusion.69
  45.6 1.3 copy.67
  46.9 11.9 %scatter_custom_fusion = f32[512,128]{1,0:T(8,128)S(1)} fusion(s32[2048]{0:T(1024)} %bitcast.104, f32[2048,128]{1,0:T(8,128)} %copy.67, f32[]{:T(128)} %constant.10.clone.1), kind=kCustom, calls=%fused_computation.83 | custom fusion | flops 262144 | bytes 262656 | tf_op jit(solution)/shard_map/jvp()/scatter-add | solution.py:101
  59.5 0.7 fusion.27
  61.5 6.2 %gather_fusion.6 = bf16[2048,128]{1,0:T(8,128)(2,1)S(1)} fusion(bf16[512,128]{1,0:T(8,128)(2,1)S(1)} %copy.70, s32[2048]{0:T(1024)S(1)} %get-tuple-element.69), kind=kCustom, calls=%fused_computation.6 | custom fusion | bytes 1056768 | tf_op jit(solution)/shard_map/transpose(jvp())/gather | solution.py:101
  67.9 0.6 multiply_reduce_fusion
  68.5 0.5 fusion.67
  69.4 0.5 copy-done.29
  69.9 0.6 fusion.13
  70.5 0.5 copy-done.7
  71.3 0.6 fusion.4
  72.1 0.5 fusion.9
  73.1 1.1 copy.77
  74.3 7.9 %all-to-all-start = ((f32[8,32,449]{2,1,0:T(8,128)}), f32[8,32,449]{2,1,0:T(8,128)S(1)}, u32[]{:S(2)}, u32[]{:S(2)}) async-start(f32[8,32,449]{2,1,0:T(8,128)} %copy.77), calls=%async_computation | async-start | bytes 1048576 | tf_op jit(solution)/shard_map/all_to_all | solution.py:24
  82.2 1.7 convolution_convert_fusion
  83.9 7.8 %all-to-all-done = f32[8,32,449]{2,1,0:T(8,128)S(1)} async-done(((f32[8,32,449]{2,1,0:T(8,128)}), f32[8,32,449]{2,1,0:T(8,128)S(1)}, u32[]{:S(2)}, u32[]{:S(2)}) %all-to-all-start) | async-done | bytes 459808 | tf_op jit(solution)/shard_map/all_to_all | solution.py:24
  91.7 0.7 reduce_sum.121
  92.3 1.5 all_to_all.17
  93.8 12.4 %all-to-all-start.1 = ((f32[32,1,449]{2,1,0:T(1,128)}), f32[32,1,449]{2,1,0:T(1,128)S(1)}, u32[]{:S(2)}, u32[]{:S(2)}) async-start(f32[32,1,449]{2,1,0:T(1,128)} %all_to_all.17), calls=%async_computation.1 | async-start | bytes 131072 | tf_op jit(solution)/shard_map/all_to_all | solution.py:31
  106.3 1.2 add_bitcast_fusion
  107.5 7.6 %all-to-all-done.1 = f32[32,1,449]{2,1,0:T(1,128)S(1)} async-done(((f32[32,1,449]{2,1,0:T(1,128)}), f32[32,1,449]{2,1,0:T(1,128)S(1)}, u32[]{:S(2)}, u32[]{:S(2)}) %all-to-all-start.1) | async-done | bytes 57504 | tf_op jit(solution)/shard_map/all_to_all | solution.py:31
  115.2 0.7 broadcast_in_dim.33
  115.8 3.9 %all-to-all-start.2 = ((f32[32,1,449]{2,1,0:T(1,128)}), f32[32,1,449]{2,1,0:T(1,128)S(1)}, u32[]{:S(2)}, u32[]{:S(2)}) async-start(f32[32,1,449]{2,1,0:T(1,128)} %broadcast_in_dim.33), calls=%async_computation.2 | async-start | bytes 131072 | tf_op jit(solution)/shard_map/all_to_all | solution.py:41
  119.7 1.2 slice_convert_fusion
  120.9 1.5 copy.73
  122.5 11.7 %scatter_custom_fusion.1 = f32[768,128]{1,0:T(8,128)S(1)} fusion(s32[2048]{0:T(1024)} %bitcast.106, f32[2048,128]{1,0:T(8,128)S(1)} %copy.73, f32[]{:T(128)} %constant.10.clone.1), kind=kCustom, calls=%fused_computation.76 | custom fusion | flops 262144 | bytes 393728 | tf_op jit(solution)/shard_map/transpose(jvp())/scatter-add | solution.py:87
  134.2 0.7 convert.12
  135.0 0.9 broadcast_in_dim.69
  135.9 5.7 %all-to-all-start.3 = ((f32[8,32,449]{2,1,0:T(8,128)}), f32[8,32,449]{2,1,0:T(8,128)S(1)}, u32[]{:S(2)}, u32[]{:S(2)}) async-start(f32[8,32,449]{2,1,0:T(8,128)} %broadcast_in_dim.69), calls=%async_computation.3 | async-start | bytes 1048576 | tf_op jit(solution)/shard_map/all_to_all | solution.py:41
  141.6 1.4 fusion.68
  143.0 1.3 collective-permute-start.7
  144.3 1.3 collective-permute-start.6
  145.6 4.6 %collective-permute-start.5 = (bf16[64,128]{1,0:T(8,128)(2,1)}, bf16[64,128]{1,0:T(8,128)(2,1)}, u32[]{:S(2)}, u32[]{:S(2)}) collective-permute-start(bf16[64,128]{1,0:T(8,128)(2,1)} %get-tuple-element.57), channel_id=1, source_target_pairs={{0,2},{2,4},{4,6},{6,8},{8,10},{10,12},{12,14},{14,16},{16,18},{18... | collective-permute-start | bytes 49160 | tf_op jit(solution)/shard_map/ppermute | solution.py:13
  150.2 10.6 %collective-permute-start.4 = (bf16[64,128]{1,0:T(8,128)(2,1)}, bf16[64,128]{1,0:T(8,128)(2,1)}, u32[]{:S(2)}, u32[]{:S(2)}) collective-permute-start(bf16[64,128]{1,0:T(8,128)(2,1)} %get-tuple-element.58), channel_id=1, source_target_pairs={{0,128},{2,130},{4,132},{6,134},{8,136},{10,138},{12,140},{14,142}... | collective-permute-start | bytes 49160 | tf_op jit(solution)/shard_map/ppermute | solution.py:13
  160.8 1.3 copy.80
  162.6 11.6 %scatter_fusion = f32[512,128]{1,0:T(8,128)S(1)} fusion(f32[512,128]{1,0:T(8,128)S(1)} %copy.75, s32[2048]{0:T(1024)S(1)} %bitcast.102, f32[2048,128]{1,0:T(8,128)S(1)} %copy.76), kind=kCustom, calls=%fused_computation.9 | custom fusion | flops 262144 | bytes 3153920 | tf_op jit(solution)/shard_map/transpose(jvp())/scatter-add | solution.py:88
  174.2 1.2 scatter_custom_fusion.3
  175.4 1.2 scatter_custom_fusion.4
  176.7 1.2 scatter_custom_fusion.5
  177.9 1.2 scatter_custom_fusion.6
  179.5 0.5 slice.76
  180.0 0.5 reshape_reshape.7
  180.5 0.7 slice_multiply_fusion.1
  181.2 0.7 slice_multiply_fusion.2
  181.9 0.7 slice_multiply_fusion
  182.6 0.5 slice_multiply_fusion.4
  (115 shorter events, 7.1 us)
Async XLA Ops:
  0.6 28.9 %copy-start.8 = (bf16[1,2048,128]{2,1,0:T(8,128)(2,1)S(1)}, bf16[1,2048,128]{2,1,0:T(8,128)(2,1)}, u32[]{:S(2)}) copy-start(bf16[1,2048,128]{2,1,0:T(8,128)(2,1)} %param.17) | copy-start | bytes 1572868
  0.6 29.1 %copy-start.9 = (bf16[1,2048,128]{2,1,0:T(8,128)(2,1)S(1)}, bf16[1,2048,128]{2,1,0:T(8,128)(2,1)}, u32[]{:S(2)}) copy-start(bf16[1,2048,128]{2,1,0:T(8,128)(2,1)} %param.15) | copy-start | bytes 1572868
  1.5 11.2 %copy-start.22 = (s32[64]{0:T(128)}, s32[64]{0:T(128)S(1)}, u32[]{:S(2)}) copy-start(s32[64]{0:T(128)S(1)} %get-tuple-element.62) | copy-start | bytes 772
  1.5 17.0 %copy-start.21 = (s32[64]{0:T(128)}, s32[64]{0:T(128)S(1)}, u32[]{:S(2)}) copy-start(s32[64]{0:T(128)S(1)} %get-tuple-element.64) | copy-start | bytes 772
  1.5 24.9 %copy-start.20 = (s32[64]{0:T(128)}, s32[64]{0:T(128)S(1)}, u32[]{:S(2)}) copy-start(s32[64]{0:T(128)S(1)} %get-tuple-element.61) | copy-start | bytes 772
  1.5 26.9 %copy-start.23 = (s32[64]{0:T(128)}, s32[64]{0:T(128)S(1)}, u32[]{:S(2)}) copy-start(s32[64]{0:T(128)S(1)} %get-tuple-element.63) | copy-start | bytes 772
  3.1 33.4 %collective-permute-start.3 = (bf16[64,128]{1,0:T(8,128)(2,1)S(1)}, bf16[64,128]{1,0:T(8,128)(2,1)S(1)}, u32[]{:S(2)}, u32[]{:S(2)}) collective-permute-start(bf16[64,128]{1,0:T(8,128)(2,1)S(1)} %gather_fusion.3), channel_id=1, source_target_pairs={{0,128},{2,130},{4,132},{6,134},{8,136},{10,138},{12,140},{14,142}... | collective-permute-start | bytes 49160 | tf_op jit(solution)/shard_map/ppermute | solution.py:13
  14.3 22.2 %collective-permute-start.1 = (bf16[64,128]{1,0:T(8,128)(2,1)S(1)}, bf16[64,128]{1,0:T(8,128)(2,1)S(1)}, u32[]{:S(2)}, u32[]{:S(2)}) collective-permute-start(bf16[64,128]{1,0:T(8,128)(2,1)S(1)} %gather_fusion.1), channel_id=1, source_target_pairs={{2,0},{4,2},{6,4},{8,6},{10,8},{12,10},{14,12},{16,14},{18,16},{20... | collective-permute-start | bytes 49160 | tf_op jit(solution)/shard_map/ppermute | solution.py:13
  15.6 14.4 %copy-start.1 = (bf16[1,512,128]{2,1,0:T(8,128)(2,1)S(1)}, bf16[1,512,128]{2,1,0:T(8,128)(2,1)}, u32[]{:S(2)}) copy-start(bf16[1,512,128]{2,1,0:T(8,128)(2,1)} %param.14) | copy-start | bytes 393220
  17.2 19.2 %collective-permute-start = (bf16[64,128]{1,0:T(8,128)(2,1)S(1)}, bf16[64,128]{1,0:T(8,128)(2,1)S(1)}, u32[]{:S(2)}, u32[]{:S(2)}) collective-permute-start(bf16[64,128]{1,0:T(8,128)(2,1)S(1)} %gather_fusion), channel_id=1, source_target_pairs={{128,0},{130,2},{132,4},{134,6},{136,8},{138,10},{140,12},{142,14}... | collective-permute-start | bytes 49160 | tf_op jit(solution)/shard_map/ppermute | solution.py:13
  20.0 16.4 %collective-permute-start.2 = (bf16[64,128]{1,0:T(8,128)(2,1)S(1)}, bf16[64,128]{1,0:T(8,128)(2,1)S(1)}, u32[]{:S(2)}, u32[]{:S(2)}) collective-permute-start(bf16[64,128]{1,0:T(8,128)(2,1)S(1)} %gather_fusion.2), channel_id=1, source_target_pairs={{0,2},{2,4},{4,6},{6,8},{8,10},{10,12},{12,14},{14,16},{16,18},{18... | collective-permute-start | bytes 49160 | tf_op jit(solution)/shard_map/ppermute | solution.py:13
  27.7 0.7 copy-start.17
  30.0 13.0 %copy-start.5 = (bf16[1,2048,128]{1,2,0:T(8,128)(2,1)}, bf16[1,2048,128]{1,2,0:T(8,128)(2,1)S(1)}, u32[]{:S(2)}) copy-start(bf16[1,2048,128]{1,2,0:T(8,128)(2,1)S(1)} %copy.64) | copy-start | bytes 1572868
  36.4 6.5 %copy-start.10 = (bf16[2048,128]{0,1:T(8,128)(2,1)}, bf16[2048,128]{0,1:T(8,128)(2,1)S(1)}, u32[]{:S(2)}) copy-start(bf16[2048,128]{0,1:T(8,128)(2,1)S(1)} %copy.66) | copy-start | bytes 1572868
  36.5 6.5 %copy-start.16 = (f32[384,128]{1,0:T(8,128)S(1)}, f32[384,128]{1,0:T(8,128)}, u32[]{:S(2)}) copy-start(f32[384,128]{1,0:T(8,128)} %param.22) | copy-start | bytes 589828
  42.9 0.8 copy-start.12
  43.0 0.9 copy-start.26
  43.9 1.0 copy-start.28
  43.9 1.4 copy-start.6
  43.9 1.4 copy-start.18
  45.6 13.3 %copy-start.14 = (f32[256,128]{1,0:T(8,128)S(1)}, f32[256,128]{1,0:T(8,128)}, u32[]{:S(2)}) copy-start(f32[256,128]{1,0:T(8,128)} %param.25) | copy-start | bytes 393220
  45.6 13.5 %copy-start.25 = (f32[128,128]{1,0:T(8,128)S(1)}, f32[128,128]{1,0:T(8,128)}, u32[]{:S(2)}) copy-start(f32[128,128]{1,0:T(8,128)} %param.26) | copy-start | bytes 196612
  46.9 12.4 %copy-start.19 = (f32[128]{0:T(128)S(1)}, f32[128]{0:T(128)}, u32[]{:S(2)}) copy-start(f32[128]{0:T(128)} %param.27) | copy-start | bytes 1540
  68.5 0.8 copy-start.2
  68.5 0.9 copy-start.27
  68.5 1.4 copy-start.29
  69.9 1.0 copy-start.7
  69.9 1.2 copy-start.11
  69.9 1.4 copy-start.13
  71.3 0.8 copy-start.15
  72.1 0.7 copy-start.24
  74.3 17.4 %all-to-all-start = ((f32[8,32,449]{2,1,0:T(8,128)}), f32[8,32,449]{2,1,0:T(8,128)S(1)}, u32[]{:S(2)}, u32[]{:S(2)}) async-start(f32[8,32,449]{2,1,0:T(8,128)} %copy.77), calls=%async_computation | async-start | bytes 1048576 | tf_op jit(solution)/shard_map/all_to_all | solution.py:24
  82.2 24.1 %copy-start.3 = (bf16[2048,128]{0,1:T(8,128)(2,1)S(1)}, bf16[2048,128]{0,1:T(8,128)(2,1)}, u32[]{:S(2)}) copy-start(bf16[2048,128]{0,1:T(8,128)(2,1)} %copy-done.2) | copy-start | bytes 1572868
  93.8 21.3 %all-to-all-start.1 = ((f32[32,1,449]{2,1,0:T(1,128)}), f32[32,1,449]{2,1,0:T(1,128)S(1)}, u32[]{:S(2)}, u32[]{:S(2)}) async-start(f32[32,1,449]{2,1,0:T(1,128)} %all_to_all.17), calls=%async_computation.1 | async-start | bytes 131072 | tf_op jit(solution)/shard_map/all_to_all | solution.py:31
  115.8 19.2 %all-to-all-start.2 = ((f32[32,1,449]{2,1,0:T(1,128)}), f32[32,1,449]{2,1,0:T(1,128)S(1)}, u32[]{:S(2)}, u32[]{:S(2)}) async-start(f32[32,1,449]{2,1,0:T(1,128)} %broadcast_in_dim.33), calls=%async_computation.2 | async-start | bytes 131072 | tf_op jit(solution)/shard_map/all_to_all | solution.py:41
  134.9 25.9 %copy-start.4 = (f32[1,2048,128]{1,2,0:T(8,128)S(1)}, f32[1,2048,128]{1,2,0:T(8,128)}, u32[]{:S(2)}) copy-start(f32[1,2048,128]{1,2,0:T(8,128)} %add_bitcast_fusion) | copy-start | bytes 3145732
  135.9 43.2 %all-to-all-start.3 = ((f32[8,32,449]{2,1,0:T(8,128)}), f32[8,32,449]{2,1,0:T(8,128)S(1)}, u32[]{:S(2)}, u32[]{:S(2)}) async-start(f32[8,32,449]{2,1,0:T(8,128)} %broadcast_in_dim.69), calls=%async_computation.3 | async-start | bytes 1048576 | tf_op jit(solution)/shard_map/all_to_all | solution.py:41
  143.0 34.9 %collective-permute-start.7 = (bf16[64,128]{1,0:T(8,128)(2,1)}, bf16[64,128]{1,0:T(8,128)(2,1)}, u32[]{:S(2)}, u32[]{:S(2)}) collective-permute-start(bf16[64,128]{1,0:T(8,128)(2,1)} %get-tuple-element.55), channel_id=1, source_target_pairs={{128,0},{130,2},{132,4},{134,6},{136,8},{138,10},{140,12},{142,14}... | collective-permute-start | bytes 49160 | tf_op jit(solution)/shard_map/ppermute | solution.py:13
  144.3 32.4 %collective-permute-start.6 = (bf16[64,128]{1,0:T(8,128)(2,1)}, bf16[64,128]{1,0:T(8,128)(2,1)}, u32[]{:S(2)}, u32[]{:S(2)}) collective-permute-start(bf16[64,128]{1,0:T(8,128)(2,1)} %get-tuple-element.56), channel_id=1, source_target_pairs={{2,0},{4,2},{6,4},{8,6},{10,8},{12,10},{14,12},{16,14},{18,16},{20... | collective-permute-start | bytes 49160 | tf_op jit(solution)/shard_map/ppermute | solution.py:13
  145.6 29.9 %collective-permute-start.5 = (bf16[64,128]{1,0:T(8,128)(2,1)}, bf16[64,128]{1,0:T(8,128)(2,1)}, u32[]{:S(2)}, u32[]{:S(2)}) collective-permute-start(bf16[64,128]{1,0:T(8,128)(2,1)} %get-tuple-element.57), channel_id=1, source_target_pairs={{0,2},{2,4},{4,6},{6,8},{8,10},{10,12},{12,14},{14,16},{16,18},{18... | collective-permute-start | bytes 49160 | tf_op jit(solution)/shard_map/ppermute | solution.py:13
  150.2 24.0 %collective-permute-start.4 = (bf16[64,128]{1,0:T(8,128)(2,1)}, bf16[64,128]{1,0:T(8,128)(2,1)}, u32[]{:S(2)}, u32[]{:S(2)}) collective-permute-start(bf16[64,128]{1,0:T(8,128)(2,1)} %get-tuple-element.58), channel_id=1, source_target_pairs={{0,128},{2,130},{4,132},{6,134},{8,136},{10,138},{12,140},{14,142}... | collective-permute-start | bytes 49160 | tf_op jit(solution)/shard_map/ppermute | solution.py:13
  179.2 2.1 %copy-start = (f32[512,128]{1,0:T(8,128)}, f32[512,128]{1,0:T(8,128)S(1)}, u32[]{:S(2)}) copy-start(f32[512,128]{1,0:T(8,128)S(1)} %scatter_custom_fusion.6) | copy-start | bytes 786436
where the time goes:
time: 187 us; the launch traced here: 183 us
  starting transfers between devices  63.8 us (34%)
  other arithmetic  53.5 us (29%)
  local copies, waits for them, and re-layouts  42.2 us (23%)
  waiting for transfers between devices  15.4 us (8%)
  matrix products  6.11 us (3%)
  between operations  2.13 us (1%)
    ppermute x8, starting transfers between devices, from_behind(): return lax.ppermute(value, axis, pairs)  33.9 us
    all_to_all x1, starting transfers between devices, sum_in_two_steps(): return jnp.sum(lax.all_to_all(own, far, 0, 0, tiled=True), axis=0)  12.4 us
    scatter-add x1, other arithmetic, local_forward(): jax.ops.segment_sum(message.astype(edges.dtype), receiving, num_segments=...  11.9 us
    scatter-add x1, other arithmetic, local_forward(): table[sending].astype(jnp.bfloat16)  11.7 us
    scatter-add x1, other arithmetic, local_forward(): cells[receiving].astype(jnp.bfloat16)  11.6 us
    all_to_all x2, starting transfers between devices, from_everyone(): lax.all_to_all(jnp.broadcast_to(value[None], (devices, *value.shape)), ax...  9.53 us
    all_to_all x1, starting transfers between devices, sent_and_summed(): lax.all_to_all(cut_along(value, dim, devices), axis, 0, 0, tiled=True)  7.91 us
    all_to_all x1, waiting for transfers between devices, sent_and_summed(): lax.all_to_all(cut_along(value, dim, devices), axis, 0, 0, tiled=True)  7.76 us
  transfers between devices with their start and end apart: 12, of which 2 were waited for; matrix products, arithmetic and copies ran while one was open for 30% of the time, Pallas kernels for 0%

commit v1 on v0

v1 whole, which is shorter than its diff:
```python
import functools

import jax
import jax.numpy as jnp
from jax import lax
from jax.experimental import pallas as pl
from jax.experimental.pallas import tpu as pltpu
from jax.sharding import PartitionSpec as P

MESH = pl.DeviceIdType.MESH
F32 = jnp.float32
BF16 = jnp.bfloat16
EDGE_TILE = 512


def nn(a, b):
    return lax.dot_general(a, b, (((1,), (0,)), ((), ())), preferred_element_type=F32)


def nt(a, b):
    return lax.dot_general(a, b, (((1,), (1,)), ((), ())), preferred_element_type=F32)


def one_hot(row, depth):
    spot = lax.broadcasted_iota(jnp.int32, (depth, row.shape[1]), 0)
    return jnp.where(spot == row, 1.0, 0.0).astype(BF16)


def sigmoid(a):
    return 0.5 * jnp.tanh(0.5 * a) + 0.5


def silu_parts(a):
    s = sigmoid(a)
    return a * s, s * (1.0 + a * (1.0 - s))


def column_of(row):
    return jnp.broadcast_to(row, (row.shape[1], row.shape[1])).T


def across(column, width):
    return jnp.concatenate([column] * (width // column.shape[1]), axis=1)


def folded(values):
    step = values.shape[0]
    return sum(values[:, i : i + step] for i in range(0, values.shape[1], step))


def row_of(partial):
    return jnp.sum(partial.T, axis=0, keepdims=True)


def normed(b):
    center = b - jnp.mean(b, axis=0, keepdims=True)
    spread = jnp.mean(center * center, axis=0, keepdims=True)
    rs = lax.rsqrt(spread + 1e-05)
    return center * rs, rs


def normed_back(dn, nh, rs):
    m1 = jnp.mean(dn, axis=0, keepdims=True)
    m2 = jnp.mean(dn * nh, axis=0, keepdims=True)
    return rs * (dn - m1 - nh * m2)


def kernel(
    sizes,
    node_hbm, edge_hbm, cotn_hbm, cote_hbm, snd, rcv, rows, cnt, w1, w2, eg, n1, n2, ng,
    gnode, gedge_hbm, gw1, gw2, geg, gn1, gn2, gng,
    h_v, e_v, cn_v, ce_v, in_sem,
    hot, tab, eT, a0, pT, dsil, nhat, rsv, daT, gT, gedge, out_sem,
    gs_send, gs_recv, gb_send, gb_recv, gsem_s, gsem_r, bsem_s, bsem_r,
    a_send, a_recv, b_send, b_recv, k_send, k_recv, zbuf, agbuf, psem_s, psem_r,
):
    peers, dps, plane, factor = sizes
    group = plane * dps
    depth = peers // plane
    C, H = h_v.shape
    E = e_v.shape[0]
    GH = rows.shape[1]
    GQ = GH // 4
    T = C + GH
    share = a_recv.shape[1]
    tiles = E // EDGE_TILE
    half = peers // 2
    last = group - 1

    m = lax.axis_index("morton")
    core = lax.axis_index("dp")
    level = m // plane
    mine = (m % plane) * dps + core
    low = m < half
    partner = lax.rem(m + half, peers)
    right = lax.rem(m + 1, peers)
    left = lax.rem(m + peers - 1, peers)

    def member(i):
        return (level * plane + i // dps, i % dps)

    def above(z):
        return (z * plane + m % plane, core)

    loads = [
        pltpu.make_async_copy(src, dst, in_sem.at[i])
        for i, (src, dst) in enumerate(((node_hbm, h_v), (edge_hbm, e_v), (cotn_hbm, cn_v), (cote_hbm, ce_v)))
    ]
    for load in loads:
        load.start()

    barrier = pltpu.get_barrier_semaphore()

    def greet(r, _):
        pl.semaphore_signal(barrier, inc=1, device_id=member(lax.rem(mine + r, group)), device_id_type=MESH)
        return 0

    lax.fori_loop(1, group, greet, 0)

    def greet_above(r, _):
        pl.semaphore_signal(barrier, inc=1, device_id=above(lax.rem(level + r, depth)), device_id_type=MESH)
        return 0

    lax.fori_loop(1, depth, greet_above, 0)
    for side in (left, right):
        pl.semaphore_signal(barrier, inc=1, device_id=(side, core), device_id_type=MESH)

    eye_r = lax.broadcasted_iota(jnp.int32, (H, H), 0)
    eye_c = lax.broadcasted_iota(jnp.int32, (H, H), 1)
    eye = jnp.where(eye_r == eye_c, 1.0, 0.0).astype(BF16)

    lane = lax.broadcasted_iota(jnp.int32, (1, GH), 1)
    first_used = jnp.logical_and(lane < GQ, jnp.logical_not(low))
    last_used = jnp.logical_and(lane >= 3 * GQ, low)
    middle = jnp.logical_and(lane >= GQ, lane < 3 * GQ)
    used = jnp.logical_or(middle, jnp.logical_or(first_used, last_used))
    hot_out = one_hot(jnp.where(used, rows[...], -1), C)

    loads[0].wait()
    hT = nt(eye, h_v[...]).astype(BF16)
    tab[:, 0:C] = hT
    picked = nn(hT, hot_out).T
    gs_send[0] = (picked[0:GQ] + picked[3 * GQ : 4 * GQ]).astype(BF16)
    gs_send[1] = picked[GQ : 2 * GQ].astype(BF16)
    gs_send[2] = picked[2 * GQ : 3 * GQ].astype(BF16)

    pl.semaphore_wait(barrier, (group - 1) + (depth - 1) + 2)

    ghost_out = [
        pltpu.make_async_remote_copy(
            src_ref=gs_send.at[k], dst_ref=gs_recv.at[k], send_sem=gsem_s.at[k], recv_sem=gsem_r.at[k],
            device_id=(to, core), device_id_type=MESH,
        )
        for k, to in enumerate((partner, left, right))
    ]
    for copy in ghost_out:
        copy.start()

    w1T = nt(eye, w1[...].astype(BF16)).astype(BF16)
    w2T = nt(eye, w2[...].astype(BF16)).astype(BF16)
    w1s_T = w1T[:, H : 2 * H]
    loads[1].wait()

    def ahead(i, _):
        cols = pl.ds(pl.multiple_of(i * EDGE_TILE, EDGE_TILE), EDGE_TILE)
        hot_s = one_hot(snd[:, cols], T)
        hot_r = one_hot(rcv[:, cols], C)
        hot[0:T, cols] = hot_s
        hot[T : T + C, cols] = hot_r
        et = nt(eye, e_v[cols, :]).astype(BF16)
        eT[:, cols] = et
        xs = nn(hT, hot_s[0:C]).astype(BF16)
        xr = nn(hT, hot_r).astype(BF16)
        a0[:, cols] = nn(w1T, jnp.concatenate([et, xs, xr], axis=0))
        return 0

    lax.fori_loop(0, tiles, ahead, 0)

    gain_e = column_of(eg[...])
    gain_n = column_of(ng[...])
    gain_tile = across(gain_e, EDGE_TILE)
    count = cnt[0, 0]

    for copy in ghost_out:
        copy.wait_recv()
    ghosts = jnp.concatenate([gs_recv[0], gs_recv[1], gs_recv[2], gs_recv[0]], axis=0)
    first_here = jnp.logical_and(lane < GQ, low)
    last_here = jnp.logical_and(lane >= 3 * GQ, jnp.logical_not(low))
    here = jnp.logical_or(middle, jnp.logical_or(first_here, last_here))
    ghost_T = jnp.where(here, nt(eye, ghosts), 0.0).astype(BF16)
    tab[:, C:T] = ghost_T

    def live_row(i):
        slot = lax.broadcasted_iota(jnp.int32, (1, EDGE_TILE), 1) + i * EDGE_TILE
        return jnp.where(slot < count, 1.0, 0.0)

    def forward(i, agg):
        cols = pl.ds(pl.multiple_of(i * EDGE_TILE, EDGE_TILE), EDGE_TILE)
        xg = nn(ghost_T, hot[C:T, cols]).astype(BF16)
        a = a0[:, cols] + nn(w1s_T, xg)
        p, d = silu_parts(a)
        p = p.astype(BF16)
        pT[:, cols] = p
        dsil[:, cols] = d
        nh, rs = normed(nn(w2T, p))
        nhat[:, cols] = nh
        rsv[:, cols] = rs
        live = live_row(i)
        msg = (live * (eT[:, cols].astype(F32) + live * (nh * gain_tile))).astype(BF16)
        return agg + nt(msg, hot[T : T + C, cols])

    agg = lax.fori_loop(0, tiles, forward, jnp.zeros((H, C), F32)).astype(BF16)

    n1b = n1[...].astype(BF16)
    n2b = n2[...].astype(BF16)
    n1T = nt(eye, n1b).astype(BF16)
    n2T = nt(eye, n2b).astype(BF16)
    loads[2].wait()
    yT = jnp.concatenate([hT, agg], axis=0)
    r, dr_ = silu_parts(nn(n1T, yT))
    r = r.astype(BF16)
    nh, rs = normed(nn(n2T, r))
    cnT = nt(eye, cn_v[...])
    acc = folded(cnT * nh)
    ds = normed_back(cnT * across(gain_n, C), nh, rs).astype(BF16)
    dc = (nn(n2b, ds).astype(BF16).astype(F32) * dr_).astype(BF16)
    dyT = nn(n1b, dc).astype(BF16)
    dagg = dyT[H:]
    b_send[0 : 2 * H] = nt(yT, dc).astype(BF16)
    b_send[2 * H : 3 * H] = nt(r, ds).astype(BF16)
    b_send[3 * H :] = jnp.zeros((b_send.shape[0] - 3 * H, H), BF16)
    gain_n_row = row_of(acc)
    node_T = cnT + dyT[0:H].astype(F32)

    def shard(i):
        return pl.ds(pl.multiple_of(i * share, share), share)

    def spread(src, dst, phase):
        def go(r, _):
            i = lax.rem(mine + r, group)
            pltpu.make_async_remote_copy(
                src_ref=src.at[shard(i)], dst_ref=dst.at[mine], send_sem=psem_s.at[phase], recv_sem=psem_r.at[phase],
                device_id=member(i), device_id_type=MESH,
            ).start()
            return 0

        lax.fori_loop(1, group, go, 0)

    def all_arrived(dst, phase, sems):
        several = dst.at[pl.ds(0, dst.shape[0] - 1)]
        pltpu.make_async_copy(several, several, sems.at[phase]).wait()

    spread(b_send, b_recv, 0)
    b_recv[mine] = b_send[shard(mine)]

    loads[3].wait()
    w2b = w2[...].astype(BF16)

    def backward(i, acc):
        cols = pl.ds(pl.multiple_of(i * EDGE_TILE, EDGE_TILE), EDGE_TILE)
        live = live_row(i)
        g = nt(eye, ce_v[cols, :]) + live * nn(dagg, hot[T : T + C, cols])
        gT[:, cols] = g
        dd = live * g
        nh = nhat[:, cols]
        acc = acc + folded(dd * nh)
        db = normed_back(dd * gain_tile, nh, rsv[:, cols]).astype(BF16)
        dp = nn(w2b, db).astype(BF16).astype(F32)
        daT[:, cols] = (dp * dsil[:, cols]).astype(BF16)
        return acc, db

    def backward_step(i, carry):
        acc, dw2 = carry
        cols = pl.ds(pl.multiple_of(i * EDGE_TILE, EDGE_TILE), EDGE_TILE)
        acc, db = backward(i, acc)
        return acc, dw2 + nt(pT[:, cols], db)

    acc, dw2 = lax.fori_loop(0, tiles, backward_step, (jnp.zeros((H, H), F32), jnp.zeros((H, H), F32)))

    da = daT[...]
    s_all = nt(hot[...], da).astype(BF16)
    a_send[0:H] = nt(eT[...], da).astype(BF16)
    a_send[H : 2 * H] = nn(tab[...], s_all[0:T]).astype(BF16)
    a_send[2 * H : 3 * H] = nn(hT, s_all[T:]).astype(BF16)
    a_send[3 * H :] = dw2.astype(BF16)
    k_send[...] = jnp.zeros_like(k_send)
    k_send[0:1] = row_of(acc).astype(BF16)
    k_send[1:2] = gain_n_row.astype(BF16)

    spread(a_send, a_recv, 1)
    a_recv[mine] = a_send[shard(mine)]

    to_last = pltpu.make_async_remote_copy(
        src_ref=k_send, dst_ref=k_recv.at[mine], send_sem=psem_s.at[2], recv_sem=psem_r.at[2],
        device_id=member(last), device_id_type=MESH,
    )

    @pl.when(mine != last)
    def _():
        to_last.start()

    w1b = w1[...].astype(BF16)
    dghost = nt(s_all[C:T], w1b[H : 2 * H])
    gb_send[0] = (dghost[0:GQ] + dghost[3 * GQ : 4 * GQ]).astype(BF16)
    gb_send[1] = dghost[GQ : 2 * GQ].astype(BF16)
    gb_send[2] = dghost[2 * GQ : 3 * GQ].astype(BF16)
    ghost_back = [
        pltpu.make_async_remote_copy(
            src_ref=gb_send.at[k], dst_ref=gb_recv.at[k], send_sem=bsem_s.at[k], recv_sem=bsem_r.at[k],
            device_id=(to, core), device_id_type=MESH,
        )
        for k, to in enumerate((partner, right, left))
    ]
    for copy in ghost_back:
        copy.start()

    def edge_out(i, _):
        cols = pl.ds(pl.multiple_of(i * EDGE_TILE, EDGE_TILE), EDGE_TILE)
        dx = nn(w1b[0:H], daT[:, cols]).astype(BF16).astype(F32)
        gedge[cols, :] = (gT[:, cols] + dx).T
        return 0

    def edge_store(i):
        cols = pl.ds(i * EDGE_TILE, EDGE_TILE)
        return pltpu.make_async_copy(gedge.at[cols], gedge_hbm.at[cols], out_sem.at[i])

    lax.fori_loop(0, tiles // 2, edge_out, 0)
    for i in range(tiles // 2):
        edge_store(i).start()

    all_arrived(a_recv, 1, psem_r)
    all_arrived(b_recv, 0, psem_r)
    zbuf[level, 0:share] = jnp.sum(a_recv[...].astype(F32), axis=0).astype(BF16)

    @pl.when(mine == last)
    def _():
        k_recv[mine] = k_send[...]
        all_arrived(k_recv, 2, psem_r)
        total = jnp.sum(k_recv[:, 0:16].astype(F32), axis=0).astype(BF16)
        zbuf[level, share : 2 * share] = jnp.zeros((share, H), BF16)
        zbuf[level, share : share + 16] = total

    @pl.when(mine != last)
    def _():
        zbuf[level, share : 2 * share] = jnp.sum(b_recv[...].astype(F32), axis=0).astype(BF16)

    def climb(r, _):
        pltpu.make_async_remote_copy(
            src_ref=zbuf.at[level], dst_ref=zbuf.at[level], send_sem=psem_s.at[3], recv_sem=psem_r.at[3],
            device_id=above(lax.rem(level + r, depth)), device_id_type=MESH,
        ).start()
        return 0

    lax.fori_loop(1, depth, climb, 0)

    lax.fori_loop(tiles // 2, tiles, edge_out, 0)
    for i in range(tiles // 2, tiles):
        edge_store(i).start()

    all_arrived(zbuf, 3, psem_r)
    agbuf[mine] = (jnp.sum(zbuf[...].astype(F32), axis=0) * factor).astype(BF16)

    def share_out(r, _):
        pltpu.make_async_remote_copy(
            src_ref=agbuf.at[mine], dst_ref=agbuf.at[mine], send_sem=psem_s.at[4], recv_sem=psem_r.at[4],
            device_id=member(lax.rem(mine + r, group)), device_id_type=MESH,
        ).start()
        return 0

    lax.fori_loop(1, group, share_out, 0)

    own = nt(s_all[0:C], w1b[H : 2 * H]).astype(BF16).astype(F32)
    own = own + nt(s_all[T:], w1b[2 * H : 3 * H]).astype(BF16).astype(F32)
    for copy in ghost_back:
        copy.wait_recv()
    back = jnp.concatenate([gb_recv[0], gb_recv[1], gb_recv[2], gb_recv[0]], axis=0)
    gnode[...] = node_T.T + own + nn(hot_out, back)

    all_arrived(agbuf, 4, psem_r)

    def landed(start, stop, offset):
        count = (stop - start) // share
        part = agbuf[start // share : start // share + count, offset : offset + share]
        return part.astype(F32).reshape(stop - start, H)

    gw1[...] = landed(0, 3 * H, 0)
    gw2[...] = landed(3 * H, 4 * H, 0)
    gn1[...] = landed(0, 2 * H, share)
    gn2[...] = landed(2 * H, 3 * H, share)
    tail = agbuf[last, share : share + 16].astype(F32)
    geg[...] = tail[0:1]
    gng[...] = tail[1:2]

    for copy in ghost_out + ghost_back:
        copy.wait_send()
    all_arrived(b_recv, 0, psem_s)
    all_arrived(a_recv, 1, psem_s)
    all_arrived(zbuf, 3, psem_s)
    all_arrived(agbuf, 4, psem_s)

    @pl.when(mine != last)
    def _():
        to_last.wait_send()

    for i in range(tiles):
        edge_store(i).wait()


def on_device(
    plane, node_feat, edge_feat, cot_node, cot_edge, senders, receivers, send_rows, edge_count,
    edge_w1, edge_w2, edge_gain, node_w1, node_w2, node_gain,
):
    peers, dps = lax.axis_size("morton"), lax.axis_size("dp")
    C, H = node_feat.shape[1:]
    E = edge_feat.shape[1]
    GH = send_rows.shape[1]
    GQ = GH // 4
    T = C + GH
    group = plane * dps
    depth = peers // plane
    share = 4 * H // group
    factor = (dps * peers * E) ** -0.5
    vmem = pl.BlockSpec(memory_space=pltpu.VMEM)
    smem = pl.BlockSpec(memory_space=pltpu.SMEM)
    hbm = pl.BlockSpec(memory_space=pl.ANY)
    shape = jax.ShapeDtypeStruct
    dma = pltpu.SemaphoreType.DMA
    tiles = E // EDGE_TILE
    outs = pl.pallas_call(
        functools.partial(kernel, (peers, dps, plane, factor)),
        out_shape=[
            shape((C, H), F32), shape((E, H), F32), shape((3 * H, H), F32), shape((H, H), F32),
            shape((1, H), F32), shape((2 * H, H), F32), shape((H, H), F32), shape((1, H), F32),
        ],
        in_specs=[hbm, hbm, hbm, hbm, vmem, vmem, vmem, smem] + [vmem] * 6,
        out_specs=[vmem, hbm] + [vmem] * 6,
        scratch_shapes=[
            pltpu.VMEM((C, H), BF16), pltpu.VMEM((E, H), BF16), pltpu.VMEM((C, H), BF16), pltpu.VMEM((E, H), BF16),
            dma((4,)),
            pltpu.VMEM((T + C, E), BF16), pltpu.VMEM((H, T), BF16), pltpu.VMEM((H, E), BF16),
            pltpu.VMEM((H, E), F32), pltpu.VMEM((H, E), BF16), pltpu.VMEM((H, E), F32), pltpu.VMEM((H, E), F32),
            pltpu.VMEM((1, E), F32), pltpu.VMEM((H, E), BF16), pltpu.VMEM((H, E), F32), pltpu.VMEM((E, H), F32),
            dma((tiles,)),
            pltpu.VMEM((3, GQ, H), BF16), pltpu.VMEM((3, GQ, H), BF16),
            pltpu.VMEM((3, GQ, H), BF16), pltpu.VMEM((3, GQ, H), BF16),
            dma((3,)), dma((3,)), dma((3,)), dma((3,)),
            pltpu.VMEM((4 * H, H), BF16), pltpu.VMEM((group, share, H), BF16),
            pltpu.VMEM((4 * H, H), BF16), pltpu.VMEM((group, share, H), BF16),
            pltpu.VMEM((16, H), BF16), pltpu.VMEM((group, 16, H), BF16),
            pltpu.VMEM((depth, 2 * share, H), BF16), pltpu.VMEM((group, 2 * share, H), BF16),
            dma((5,)), dma((5,)),
        ],
        compiler_params=pltpu.CompilerParams(
            collective_id=0, has_side_effects=True, vmem_limit_bytes=40 * 1024 * 1024
        ),
    )(
        node_feat[0], edge_feat[0], cot_node[0], cot_edge[0], senders, receivers, send_rows, edge_count,
        edge_w1, edge_w2, edge_gain.reshape(1, H), node_w1, node_w2, node_gain.reshape(1, H),
    )
    return (
        outs[0][None], outs[1][None], outs[2], outs[3], outs[4].reshape(H), outs[5], outs[6], outs[7].reshape(H)
    )


def solution(mesh):
    cells = P("dp", "morton", None)
    flat = P("dp", "morton")
    plane = min(16, mesh.shape["morton"] // 2)
    return jax.shard_map(
        functools.partial(on_device, plane),
        mesh=mesh,
        in_specs=(cells, cells, cells, cells, flat, flat, flat, flat, P(), P(), P(), P(), P(), P()),
        out_specs=(cells, cells, P(), P(), P(), P(), P(), P()),
        check_vma=False,
    )
```

time: 187 us -> 59.7 us (0.32); the launches traced: 183 us -> 59.3 us
  starting transfers between devices: 63.8 us -> 0 us
  other arithmetic: 53.5 us -> 0 us
  Pallas kernels: 0 us -> 43.9 us
  local copies, waits for them, and re-layouts: 42.2 us -> 14 us
  waiting for transfers between devices: 15.4 us -> 0 us
  matrix products: 6.11 us -> 0 us
    pallas_call x0 -> x1, Pallas kernels: none -> 43.9 us  [on_device(): pl.pallas_call(functools.partial(kernel, (peers, dps, plane, factor)), ou...]
    scatter-add x7 -> x0, other arithmetic: 40 us -> none  [the longest x1 11.9 us: local_forward(): jax.ops.segment_sum(message.astype(edges.dtype), receiving, num_segments=...]
    ppermute x8 -> x0, starting transfers between devices: 33.9 us -> none  [from_behind(): return lax.ppermute(value, axis, pairs)]
    all_to_all x4 -> x0, starting transfers between devices: 29.9 us -> none  [the longest x1 12.4 us: sum_in_two_steps(): return jnp.sum(lax.all_to_all(own, far, 0, 0, tiled=True), axis=0)]
    gather x10 -> x0, local copies, waits for them, and re-layouts: 25.4 us -> none  [the longest x2 6.4 us: local_forward(): jax.ops.segment_sum(message.astype(edges.dtype), receiving, num_segments=...]
    all_to_all x4 -> x0, waiting for transfers between devices: 15.4 us -> none  [the longest x1 7.76 us: sent_and_summed(): lax.all_to_all(cut_along(value, dim, devices), axis, 0, 0, tiled=True)]
    unnamed x69 -> x34, local copies, waits for them, and re-layouts: 6.04 us -> 14 us
    dot_general x12 -> x0, matrix products: 6.11 us -> none  [the longest x3 2.9 us: local_forward(): jnp.dot(joined, ew1.astype(jnp.bfloat16), preferred_element_type=jnp.floa...]
  transfers between devices with their start and end apart: 12 -> 0, of which waited for: 2 -> 0; matrix products, arithmetic and copies ran while one was open for 30% -> 0% of each run, Pallas kernels for 0% -> 0%
where the time goes in v1:
time: 59.7 us; the launch traced here: 59.3 us
  Pallas kernels  43.9 us (74%)
  local copies, waits for them, and re-layouts  14 us (23%)
  between operations  1.36 us (2%)
    pallas_call x1, Pallas kernels, on_device(): pl.pallas_call(functools.partial(kernel, (peers, dps, plane, factor)), ou...  43.9 us
    unnamed x34, local copies, waits for them, and re-layouts  14 us

profile of v1, /device:TPU:1, one launch (start us, length us, event | category | flops | bytes accessed | tf_op | source)
XLA Modules:
  0.0 59.3 jit_solution(3898638775940564763)
XLA Ops:
  0.6 0.0 copy-start.8
  1.3 0.0 copy-start.12
  1.3 0.0 copy-start.10
  1.3 0.0 copy-start.11
  1.3 0.0 copy-done.8
  1.3 0.6 %copy-done.12 = f32[128]{0:T(128)S(1)} copy-done((f32[128]{0:T(128)S(1)}, f32[128]{0:T(128)}, u32[]{:S(2)}) %copy-start.12) | copy-done | bytes 536
  2.0 0.0 copy-done.10
  2.0 0.0 copy-done.11
  2.0 0.0 copy-start
  2.0 1.0 %copy-done = bf16[1,2048,128]{2,1,0:T(8,128)(2,1)S(1)} copy-done((bf16[1,2048,128]{2,1,0:T(8,128)(2,1)S(1)}, bf16[1,2048,128]{2,1,0:T(8,128)(2,1)}, u32[]{:S(2)}) %copy-start) | copy-done | bytes 524312
  3.0 0.0 copy-start.1
  3.1 1.0 %copy-done.1 = bf16[1,2048,128]{2,1,0:T(8,128)(2,1)S(1)} copy-done((bf16[1,2048,128]{2,1,0:T(8,128)(2,1)S(1)}, bf16[1,2048,128]{2,1,0:T(8,128)(2,1)}, u32[]{:S(2)}) %copy-start.1) | copy-done | bytes 524312
  4.1 0.0 copy-start.2
  4.1 0.9 %copy-done.2 = f32[384,128]{1,0:T(8,128)S(1)} copy-done((f32[384,128]{1,0:T(8,128)S(1)}, f32[384,128]{1,0:T(8,128)}, u32[]{:S(2)}) %copy-start.2) | copy-done | bytes 196632
  5.0 0.0 copy-start.3
  5.0 0.9 %copy-done.3 = bf16[1,512,128]{2,1,0:T(8,128)(2,1)S(1)} copy-done((bf16[1,512,128]{2,1,0:T(8,128)(2,1)S(1)}, bf16[1,512,128]{2,1,0:T(8,128)(2,1)}, u32[]{:S(2)}) %copy-start.3) | copy-done | bytes 131096
  5.9 0.0 copy-start.4
  5.9 0.9 %copy-done.4 = bf16[1,512,128]{2,1,0:T(8,128)(2,1)S(1)} copy-done((bf16[1,512,128]{2,1,0:T(8,128)(2,1)S(1)}, bf16[1,512,128]{2,1,0:T(8,128)(2,1)}, u32[]{:S(2)}) %copy-start.4) | copy-done | bytes 131096
  6.8 0.0 copy-start.5
  6.8 0.9 %copy-done.5 = f32[256,128]{1,0:T(8,128)S(1)} copy-done((f32[256,128]{1,0:T(8,128)S(1)}, f32[256,128]{1,0:T(8,128)}, u32[]{:S(2)}) %copy-start.5) | copy-done | bytes 131096
  7.7 0.0 copy-start.6
  7.7 0.8 %copy-done.6 = f32[128,128]{1,0:T(8,128)S(1)} copy-done((f32[128,128]{1,0:T(8,128)S(1)}, f32[128,128]{1,0:T(8,128)}, u32[]{:S(2)}) %copy-start.6) | copy-done | bytes 65560
  8.6 0.0 copy-start.7
  8.6 0.8 %copy-done.7 = f32[128,128]{1,0:T(8,128)S(1)} copy-done((f32[128,128]{1,0:T(8,128)S(1)}, f32[128,128]{1,0:T(8,128)}, u32[]{:S(2)}) %copy-start.7) | copy-done | bytes 65560
  9.4 0.0 copy-start.9
  9.4 0.7 %copy-done.9 = s32[1,2048]{1,0:T(1,128)S(1)} copy-done((s32[1,2048]{1,0:T(1,128)S(1)}, s32[1,2048]{1,0:T(1,128)}, u32[]{:S(2)}) %copy-start.9) | copy-done | bytes 8216
  10.1 43.9 %shard_map.197 = (f32[512,128]{1,0:T(8,128)S(1)}, f32[2048,128]{1,0:T(8,128)S(1)}, f32[384,128]{1,0:T(8,128)S(1)}, f32[128,128]{1,0:T(8,128)S(1)}, f32[1,128]{1,...) custom-call(bf16[512,128]{1,0:T(8,128)(2,1)S(1)} %bitcast.14, ...), custom_call_target="tpu_custom_call" | custom-call | tf_op jit(solution)/shard_map/pallas_call | solution.py:429
  54.0 0.7 %copy.31 = f32[1,512,128]{2,1,0:T(8,128)} copy(f32[1,512,128]{2,1,0:T(8,128)S(1)} %bitcast.13) | data formatting | bytes 524288
  54.7 1.0 %copy.32 = f32[1,2048,128]{2,1,0:T(8,128)} copy(f32[1,2048,128]{2,1,0:T(8,128)S(1)} %bitcast.10) | data formatting | bytes 2097152
  55.7 0.7 %copy.33 = f32[384,128]{1,0:T(8,128)} copy(f32[384,128]{1,0:T(8,128)S(1)} %get-tuple-element.34) | data formatting | bytes 393216
  56.4 0.6 %copy.34 = f32[128,128]{1,0:T(8,128)} copy(f32[128,128]{1,0:T(8,128)S(1)} %get-tuple-element.35) | data formatting | bytes 131072
  57.0 0.5 copy.35
  57.5 0.7 %copy.36 = f32[256,128]{1,0:T(8,128)} copy(f32[256,128]{1,0:T(8,128)S(1)} %get-tuple-element.37) | data formatting | bytes 262144
  58.1 0.6 %copy.37 = f32[128,128]{1,0:T(8,128)} copy(f32[128,128]{1,0:T(8,128)S(1)} %get-tuple-element.38) | data formatting | bytes 131072
  58.8 0.5 copy.38
Async XLA Ops:
  0.6 0.7 %copy-start.8 = (s32[1,2048]{1,0:T(1,128)S(1)}, s32[1,2048]{1,0:T(1,128)}, u32[]{:S(2)}) copy-start(s32[1,2048]{1,0:T(1,128)} %snd.1) | copy-start | bytes 24580
  1.3 0.7 %copy-start.12 = (f32[128]{0:T(128)S(1)}, f32[128]{0:T(128)}, u32[]{:S(2)}) copy-start(f32[128]{0:T(128)} %param.27) | copy-start | bytes 1540
  1.3 0.7 %copy-start.10 = (s32[1,256]{1,0:T(1,128)S(1)}, s32[1,256]{1,0:T(1,128)}, u32[]{:S(2)}) copy-start(s32[1,256]{1,0:T(1,128)} %rows.1) | copy-start | bytes 3076
  1.3 0.7 %copy-start.11 = (f32[128]{0:T(128)S(1)}, f32[128]{0:T(128)}, u32[]{:S(2)}) copy-start(f32[128]{0:T(128)} %param.24) | copy-start | bytes 1540
  2.0 1.0 %copy-start = (bf16[1,2048,128]{2,1,0:T(8,128)(2,1)S(1)}, bf16[1,2048,128]{2,1,0:T(8,128)(2,1)}, u32[]{:S(2)}) copy-start(bf16[1,2048,128]{2,1,0:T(8,128)(2,1)} %param.15) | copy-start | bytes 1572868
  3.0 1.0 %copy-start.1 = (bf16[1,2048,128]{2,1,0:T(8,128)(2,1)S(1)}, bf16[1,2048,128]{2,1,0:T(8,128)(2,1)}, u32[]{:S(2)}) copy-start(bf16[1,2048,128]{2,1,0:T(8,128)(2,1)} %param.17) | copy-start | bytes 1572868
  4.1 0.9 %copy-start.2 = (f32[384,128]{1,0:T(8,128)S(1)}, f32[384,128]{1,0:T(8,128)}, u32[]{:S(2)}) copy-start(f32[384,128]{1,0:T(8,128)} %w1.1) | copy-start | bytes 589828
  5.0 0.9 %copy-start.3 = (bf16[1,512,128]{2,1,0:T(8,128)(2,1)S(1)}, bf16[1,512,128]{2,1,0:T(8,128)(2,1)}, u32[]{:S(2)}) copy-start(bf16[1,512,128]{2,1,0:T(8,128)(2,1)} %param.14) | copy-start | bytes 393220
  5.9 0.9 %copy-start.4 = (bf16[1,512,128]{2,1,0:T(8,128)(2,1)S(1)}, bf16[1,512,128]{2,1,0:T(8,128)(2,1)}, u32[]{:S(2)}) copy-start(bf16[1,512,128]{2,1,0:T(8,128)(2,1)} %param.16) | copy-start | bytes 393220
  6.8 0.9 %copy-start.5 = (f32[256,128]{1,0:T(8,128)S(1)}, f32[256,128]{1,0:T(8,128)}, u32[]{:S(2)}) copy-start(f32[256,128]{1,0:T(8,128)} %n1.1) | copy-start | bytes 393220
  7.7 0.8 %copy-start.6 = (f32[128,128]{1,0:T(8,128)S(1)}, f32[128,128]{1,0:T(8,128)}, u32[]{:S(2)}) copy-start(f32[128,128]{1,0:T(8,128)} %w2.1) | copy-start | bytes 196612
  8.6 0.8 %copy-start.7 = (f32[128,128]{1,0:T(8,128)S(1)}, f32[128,128]{1,0:T(8,128)}, u32[]{:S(2)}) copy-start(f32[128,128]{1,0:T(8,128)} %n2.1) | copy-start | bytes 196612
  9.4 0.7 %copy-start.9 = (s32[1,2048]{1,0:T(1,128)S(1)}, s32[1,2048]{1,0:T(1,128)}, u32[]{:S(2)}) copy-start(s32[1,2048]{1,0:T(1,128)} %rcv.1) | copy-start | bytes 24580

commit v2 on v1

--- a/solution.py
+++ b/solution.py
@@ -67,10 +67,11 @@
 
 def kernel(
     sizes,
-    node_hbm, edge_hbm, cotn_hbm, cote_hbm, snd, rcv, rows, cnt, w1, w2, eg, n1, n2, ng,
-    gnode, gedge_hbm, gw1, gw2, geg, gn1, gn2, gng,
-    h_v, e_v, cn_v, ce_v, in_sem,
-    hot, tab, eT, a0, pT, dsil, nhat, rsv, daT, gT, gedge, out_sem,
+    node_hbm, rows_hbm, edge_hbm, snd_hbm, rcv_hbm, w1_hbm, w2_hbm, cnt_hbm,
+    eg_hbm, ng_hbm, n1_hbm, n2_hbm, cotn_hbm, cote_hbm,
+    gnode, gedge, gw1, gw2, geg, gn1, gn2, gng,
+    h_v, rows, e_v, snd, rcv, w1, w2, cnt, eg, ng, n1, n2, cn_v, ce_v, in_sem,
+    hot, tab, eT, a0, pT, dsil, nhat, rsv, daT, gT,
     gs_send, gs_recv, gb_send, gb_recv, gsem_s, gsem_r, bsem_s, bsem_r,
     a_send, a_recv, b_send, b_recv, k_send, k_recv, zbuf, agbuf, psem_s, psem_r,
 ):
@@ -102,9 +103,13 @@
     def above(z):
         return (z * plane + m % plane, core)
 
+    sources = (
+        node_hbm, rows_hbm, edge_hbm, snd_hbm, rcv_hbm, w1_hbm, w2_hbm, cnt_hbm,
+        eg_hbm, ng_hbm, n1_hbm, n2_hbm, cotn_hbm, cote_hbm,
+    )
+    places = (h_v, rows, e_v, snd, rcv, w1, w2, cnt, eg, ng, n1, n2, cn_v, ce_v)
     loads = [
-        pltpu.make_async_copy(src, dst, in_sem.at[i])
-        for i, (src, dst) in enumerate(((node_hbm, h_v), (edge_hbm, e_v), (cotn_hbm, cn_v), (cote_hbm, ce_v)))
+        pltpu.make_async_copy(src, dst, in_sem.at[i]) for i, (src, dst) in enumerate(zip(sources, places))
     ]
     for load in loads:
         load.start()
@@ -134,9 +139,10 @@
     last_used = jnp.logical_and(lane >= 3 * GQ, low)
     middle = jnp.logical_and(lane >= GQ, lane < 3 * GQ)
     used = jnp.logical_or(middle, jnp.logical_or(first_used, last_used))
+    loads[0].wait()
+    loads[1].wait()
     hot_out = one_hot(jnp.where(used, rows[...], -1), C)
 
-    loads[0].wait()
     hT = nt(eye, h_v[...]).astype(BF16)
     tab[:, 0:C] = hT
     picked = nn(hT, hot_out).T
@@ -156,10 +162,11 @@
     for copy in ghost_out:
         copy.start()
 
+    for load in loads[2:7]:
+        load.wait()
     w1T = nt(eye, w1[...].astype(BF16)).astype(BF16)
     w2T = nt(eye, w2[...].astype(BF16)).astype(BF16)
     w1s_T = w1T[:, H : 2 * H]
-    loads[1].wait()
 
     def ahead(i, _):
         cols = pl.ds(pl.multiple_of(i * EDGE_TILE, EDGE_TILE), EDGE_TILE)
@@ -176,6 +183,8 @@
 
     lax.fori_loop(0, tiles, ahead, 0)
 
+    for load in loads[7:12]:
+        load.wait()
     gain_e = column_of(eg[...])
     gain_n = column_of(ng[...])
     gain_tile = across(gain_e, EDGE_TILE)
@@ -215,7 +224,7 @@
     n2b = n2[...].astype(BF16)
     n1T = nt(eye, n1b).astype(BF16)
     n2T = nt(eye, n2b).astype(BF16)
-    loads[2].wait()
+    loads[12].wait()
     yT = jnp.concatenate([hT, agg], axis=0)
     r, dr_ = silu_parts(nn(n1T, yT))
     r = r.astype(BF16)
@@ -253,7 +262,7 @@
     spread(b_send, b_recv, 0)
     b_recv[mine] = b_send[shard(mine)]
 
-    loads[3].wait()
+    loads[13].wait()
     w2b = w2[...].astype(BF16)
 
     def backward(i, acc):
@@ -320,13 +329,7 @@
         gedge[cols, :] = (gT[:, cols] + dx).T
         return 0
 
-    def edge_store(i):
-        cols = pl.ds(i * EDGE_TILE, EDGE_TILE)
-        return pltpu.make_async_copy(gedge.at[cols], gedge_hbm.at[cols], out_sem.at[i])
-
     lax.fori_loop(0, tiles // 2, edge_out, 0)
-    for i in range(tiles // 2):
-        edge_store(i).start()
 
     all_arrived(a_recv, 1, psem_r)
     all_arrived(b_recv, 0, psem_r)
@@ -354,8 +357,6 @@
     lax.fori_loop(1, depth, climb, 0)
 
     lax.fori_loop(tiles // 2, tiles, edge_out, 0)
-    for i in range(tiles // 2, tiles):
-        edge_store(i).start()
 
     all_arrived(zbuf, 3, psem_r)
     agbuf[mine] = (jnp.sum(zbuf[...].astype(F32), axis=0) * factor).astype(BF16)
@@ -402,8 +403,15 @@
     def _():
         to_last.wait_send()
 
-    for i in range(tiles):
-        edge_store(i).wait()
+
+def deliver(*refs):
+    n = len(refs) // 2
+    sem = refs[-1]
+    copies = [pltpu.make_async_copy(refs[i], refs[n + i], sem.at[i]) for i in range(n)]
+    for copy in copies:
+        copy.start()
+    for copy in copies:
+        copy.wait()
 
 
 def on_device(
@@ -421,26 +429,30 @@
     share = 4 * H // group
     factor = (dps * peers * E) ** -0.5
     vmem = pl.BlockSpec(memory_space=pltpu.VMEM)
-    smem = pl.BlockSpec(memory_space=pltpu.SMEM)
-    hbm = pl.BlockSpec(memory_space=pl.ANY)
+    hbm = pl.BlockSpec(memory_space=pltpu.HBM)
     shape = jax.ShapeDtypeStruct
     dma = pltpu.SemaphoreType.DMA
-    tiles = E // EDGE_TILE
+    results = [
+        shape((C, H), F32), shape((E, H), F32), shape((3 * H, H), F32), shape((H, H), F32),
+        shape((1, H), F32), shape((2 * H, H), F32), shape((H, H), F32), shape((1, H), F32),
+    ]
+    args = [
+        node_feat[0], send_rows, edge_feat[0], senders, receivers, edge_w1, edge_w2, edge_count,
+        edge_gain.reshape(1, H), node_gain.reshape(1, H), node_w1, node_w2, cot_node[0], cot_edge[0],
+    ]
+    args = [a if a is edge_count else pltpu.with_memory_space_constraint(a, pltpu.HBM) for a in args]
+    landing = [pltpu.VMEM(a.shape, a.dtype) for a in args]
+    landing[7] = pltpu.SMEM((1, 1), jnp.int32)
     outs = pl.pallas_call(
         functools.partial(kernel, (peers, dps, plane, factor)),
-        out_shape=[
-            shape((C, H), F32), shape((E, H), F32), shape((3 * H, H), F32), shape((H, H), F32),
-            shape((1, H), F32), shape((2 * H, H), F32), shape((H, H), F32), shape((1, H), F32),
-        ],
-        in_specs=[hbm, hbm, hbm, hbm, vmem, vmem, vmem, smem] + [vmem] * 6,
-        out_specs=[vmem, hbm] + [vmem] * 6,
-        scratch_shapes=[
-            pltpu.VMEM((C, H), BF16), pltpu.VMEM((E, H), BF16), pltpu.VMEM((C, H), BF16), pltpu.VMEM((E, H), BF16),
-            dma((4,)),
+        out_shape=results,
+        in_specs=[hbm] * 14,
+        out_specs=[vmem] * 8,
+        scratch_shapes=landing + [
+            dma((14,)),
             pltpu.VMEM((T + C, E), BF16), pltpu.VMEM((H, T), BF16), pltpu.VMEM((H, E), BF16),
             pltpu.VMEM((H, E), F32), pltpu.VMEM((H, E), BF16), pltpu.VMEM((H, E), F32), pltpu.VMEM((H, E), F32),
-            pltpu.VMEM((1, E), F32), pltpu.VMEM((H, E), BF16), pltpu.VMEM((H, E), F32), pltpu.VMEM((E, H), F32),
-            dma((tiles,)),
+            pltpu.VMEM((1, E), F32), pltpu.VMEM((H, E), BF16), pltpu.VMEM((H, E), F32),
             pltpu.VMEM((3, GQ, H), BF16), pltpu.VMEM((3, GQ, H), BF16),
             pltpu.VMEM((3, GQ, H), BF16), pltpu.VMEM((3, GQ, H), BF16),
             dma((3,)), dma((3,)), dma((3,)), dma((3,)),
@@ -453,10 +465,15 @@
         compiler_params=pltpu.CompilerParams(
             collective_id=0, has_side_effects=True, vmem_limit_bytes=40 * 1024 * 1024
         ),
-    )(
-        node_feat[0], edge_feat[0], cot_node[0], cot_edge[0], senders, receivers, send_rows, edge_count,
-        edge_w1, edge_w2, edge_gain.reshape(1, H), node_w1, node_w2, node_gain.reshape(1, H),
-    )
+    )(*args)
+    outs = [pltpu.with_memory_space_constraint(a, pltpu.VMEM) for a in outs]
+    outs = pl.pallas_call(
+        deliver,
+        out_shape=results,
+        in_specs=[vmem] * 8,
+        out_specs=[hbm] * 8,
+        scratch_shapes=[dma((8,))],
+    )(*outs)
     return (
         outs[0][None], outs[1][None], outs[2], outs[3], outs[4].reshape(H), outs[5], outs[6], outs[7].reshape(H)
     )

time: 59.7 us -> 46.1 us (0.77)
  local copies, waits for them, and re-layouts: 14 us -> 0 us
  Pallas kernels: 43.9 us -> 44.7 us
    unnamed x34 -> x0, local copies, waits for them, and re-layouts: 14 us -> none
    pallas_call x0 -> x1, Pallas kernels: none -> 1.27 us  [on_device(): pl.pallas_call(deliver, out_shape=results, in_specs=[vmem] * 8, out_specs...]
where the time goes in v2:
time: 46.1 us; the launch traced here: 46 us
  Pallas kernels  44.7 us (97%)
  between operations  1.29 us (3%)
    pallas_call x1, Pallas kernels, on_device(): pl.pallas_call(functools.partial(kernel, (peers, dps, plane, factor)), ou...  43.5 us
    pallas_call x1, Pallas kernels, on_device(): pl.pallas_call(deliver, out_shape=results, in_specs=[vmem] * 8, out_specs...  1.27 us

profile of v2, /device:TPU:1, one launch (start us, length us, event | category | flops | bytes accessed | tf_op | source)
XLA Modules:
  0.0 46.0 jit_solution(2224880044381295757)
XLA Ops:
  1.3 43.5 %shard_map.197 = (f32[512,128]{1,0:T(8,128)S(1)}, f32[2048,128]{1,0:T(8,128)S(1)}, f32[384,128]{1,0:T(8,128)S(1)}, f32[128,128]{1,0:T(8,128)S(1)}, f32[1,128]{1,...) custom-call(bf16[512,128]{1,0:T(8,128)(2,1)} %bitcast.12, ...), custom_call_target="tpu_custom_call" | custom-call | tf_op jit(solution)/shard_map/pallas_call | solution.py:446
  44.8 1.3 %shard_map.198 = (f32[512,128]{1,0:T(8,128)}, f32[2048,128]{1,0:T(8,128)}, f32[384,128]{1,0:T(8,128)}, f32[128,128]{1,0:T(8,128)}, f32[1,128]{1,0:T(1,128)}, /*i...) custom-call(f32[512,128]{1,0:T(8,128)S(1)} %get-tuple-element.24.refs_0_, ...), custom_call_target="tpu_custom_call" | custom-call | tf_op jit(solution)/shard_map/pallas_call | solution.py:470

commit v3 on v2

--- a/solution.py
+++ b/solution.py
@@ -10,7 +10,7 @@
 MESH = pl.DeviceIdType.MESH
 F32 = jnp.float32
 BF16 = jnp.bfloat16
-EDGE_TILE = 512
+GAIN_ROWS = 16
 
 
 def nn(a, b):
@@ -71,9 +71,9 @@
     eg_hbm, ng_hbm, n1_hbm, n2_hbm, cotn_hbm, cote_hbm,
     gnode, gedge, gw1, gw2, geg, gn1, gn2, gng,
     h_v, rows, e_v, snd, rcv, w1, w2, cnt, eg, ng, n1, n2, cn_v, ce_v, in_sem,
-    hot, tab, eT, a0, pT, dsil, nhat, rsv, daT, gT,
+    hot, tab, dsil, nhat, gT,
     gs_send, gs_recv, gb_send, gb_recv, gsem_s, gsem_r, bsem_s, bsem_r,
-    a_send, a_recv, b_send, b_recv, k_send, k_recv, zbuf, agbuf, psem_s, psem_r,
+    a_send, a_recv, a_lift, a_all, b_send, b_recv, b_lift, b_all, psem_s, psem_r,
 ):
     peers, dps, plane, factor = sizes
     group = plane * dps
@@ -83,8 +83,7 @@
     GH = rows.shape[1]
     GQ = GH // 4
     T = C + GH
-    share = a_recv.shape[1]
-    tiles = E // EDGE_TILE
+    share = b_recv.shape[1]
     half = peers // 2
     last = group - 1
 
@@ -168,26 +167,20 @@
     w2T = nt(eye, w2[...].astype(BF16)).astype(BF16)
     w1s_T = w1T[:, H : 2 * H]
 
-    def ahead(i, _):
-        cols = pl.ds(pl.multiple_of(i * EDGE_TILE, EDGE_TILE), EDGE_TILE)
-        hot_s = one_hot(snd[:, cols], T)
-        hot_r = one_hot(rcv[:, cols], C)
-        hot[0:T, cols] = hot_s
-        hot[T : T + C, cols] = hot_r
-        et = nt(eye, e_v[cols, :]).astype(BF16)
-        eT[:, cols] = et
-        xs = nn(hT, hot_s[0:C]).astype(BF16)
-        xr = nn(hT, hot_r).astype(BF16)
-        a0[:, cols] = nn(w1T, jnp.concatenate([et, xs, xr], axis=0))
-        return 0
-
-    lax.fori_loop(0, tiles, ahead, 0)
+    hot_s = one_hot(snd[...], T)
+    hot_r = one_hot(rcv[...], C)
+    hot[0:T] = hot_s
+    hot[T : T + C] = hot_r
+    eT = nt(eye, e_v[...]).astype(BF16)
+    xs = nn(hT, hot_s[0:C]).astype(BF16)
+    xr = nn(hT, hot_r).astype(BF16)
+    a0 = nn(w1T, jnp.concatenate([eT, xs, xr], axis=0))
 
     for load in loads[7:12]:
         load.wait()
     gain_e = column_of(eg[...])
     gain_n = column_of(ng[...])
-    gain_tile = across(gain_e, EDGE_TILE)
+    gain_tile = across(gain_e, E)
     count = cnt[0, 0]
 
     for copy in ghost_out:
@@ -199,26 +192,17 @@
     ghost_T = jnp.where(here, nt(eye, ghosts), 0.0).astype(BF16)
     tab[:, C:T] = ghost_T
 
-    def live_row(i):
-        slot = lax.broadcasted_iota(jnp.int32, (1, EDGE_TILE), 1) + i * EDGE_TILE
-        return jnp.where(slot < count, 1.0, 0.0)
-
-    def forward(i, agg):
-        cols = pl.ds(pl.multiple_of(i * EDGE_TILE, EDGE_TILE), EDGE_TILE)
-        xg = nn(ghost_T, hot[C:T, cols]).astype(BF16)
-        a = a0[:, cols] + nn(w1s_T, xg)
-        p, d = silu_parts(a)
-        p = p.astype(BF16)
-        pT[:, cols] = p
-        dsil[:, cols] = d
-        nh, rs = normed(nn(w2T, p))
-        nhat[:, cols] = nh
-        rsv[:, cols] = rs
-        live = live_row(i)
-        msg = (live * (eT[:, cols].astype(F32) + live * (nh * gain_tile))).astype(BF16)
-        return agg + nt(msg, hot[T : T + C, cols])
-
-    agg = lax.fori_loop(0, tiles, forward, jnp.zeros((H, C), F32)).astype(BF16)
+    slot = lax.broadcasted_iota(jnp.int32, (1, E), 1)
+    live = jnp.where(slot < count, 1.0, 0.0)
+
+    xg = nn(ghost_T, hot[C:T]).astype(BF16)
+    p, d = silu_parts(a0 + nn(w1s_T, xg))
+    pT = p.astype(BF16)
+    dsil[...] = d
+    nh, e_rs = normed(nn(w2T, pT))
+    nhat[...] = nh
+    msg = (live * (eT.astype(F32) + live * (nh * gain_tile))).astype(BF16)
+    agg = nt(msg, hot[T : T + C]).astype(BF16)
 
     n1b = n1[...].astype(BF16)
     n2b = n2[...].astype(BF16)
@@ -244,69 +228,83 @@
     def shard(i):
         return pl.ds(pl.multiple_of(i * share, share), share)
 
-    def spread(src, dst, phase):
+    def push(src, dst, phase, to):
+        pltpu.make_async_remote_copy(
+            src_ref=src, dst_ref=dst, send_sem=psem_s.at[phase], recv_sem=psem_r.at[phase],
+            device_id=to, device_id_type=MESH,
+        ).start()
+
+    def await_bytes(ref, sem):
+        pltpu.make_async_copy(ref, ref, sem).wait()
+
+    def each_member(act):
         def go(r, _):
-            i = lax.rem(mine + r, group)
-            pltpu.make_async_remote_copy(
-                src_ref=src.at[shard(i)], dst_ref=dst.at[mine], send_sem=psem_s.at[phase], recv_sem=psem_r.at[phase],
-                device_id=member(i), device_id_type=MESH,
-            ).start()
+            act(lax.rem(mine + r, group))
             return 0
 
         lax.fori_loop(1, group, go, 0)
 
-    def all_arrived(dst, phase, sems):
-        several = dst.at[pl.ds(0, dst.shape[0] - 1)]
-        pltpu.make_async_copy(several, several, sems.at[phase]).wait()
-
-    spread(b_send, b_recv, 0)
+    def each_level(act):
+        def go(r, _):
+            act(lax.rem(level + r, depth))
+            return 0
+
+        lax.fori_loop(1, depth, go, 0)
+
+    b_others = b_recv.at[pl.ds(0, group - 1)]
+    b_levels = b_lift.at[pl.ds(0, depth - 1)]
+    b_shares = b_all.at[pl.ds(0, group - 1)]
+
+    each_member(lambda i: push(b_send.at[shard(i)], b_recv.at[mine], 0, member(i)))
     b_recv[mine] = b_send[shard(mine)]
 
     loads[13].wait()
     w2b = w2[...].astype(BF16)
-
-    def backward(i, acc):
-        cols = pl.ds(pl.multiple_of(i * EDGE_TILE, EDGE_TILE), EDGE_TILE)
-        live = live_row(i)
-        g = nt(eye, ce_v[cols, :]) + live * nn(dagg, hot[T : T + C, cols])
-        gT[:, cols] = g
-        dd = live * g
-        nh = nhat[:, cols]
-        acc = acc + folded(dd * nh)
-        db = normed_back(dd * gain_tile, nh, rsv[:, cols]).astype(BF16)
-        dp = nn(w2b, db).astype(BF16).astype(F32)
-        daT[:, cols] = (dp * dsil[:, cols]).astype(BF16)
-        return acc, db
-
-    def backward_step(i, carry):
-        acc, dw2 = carry
-        cols = pl.ds(pl.multiple_of(i * EDGE_TILE, EDGE_TILE), EDGE_TILE)
-        acc, db = backward(i, acc)
-        return acc, dw2 + nt(pT[:, cols], db)
-
-    acc, dw2 = lax.fori_loop(0, tiles, backward_step, (jnp.zeros((H, H), F32), jnp.zeros((H, H), F32)))
-
-    da = daT[...]
+    g = nt(eye, ce_v[...]) + live * nn(dagg, hot[T : T + C])
+    gT[...] = g
+    dd = live * g
+    nh = nhat[...]
+    acc = folded(dd * nh)
+    db = normed_back(dd * gain_tile, nh, e_rs).astype(BF16)
+    dp = nn(w2b, db).astype(BF16).astype(F32)
+    da = (dp * dsil[...]).astype(BF16)
+
+    await_bytes(b_others, psem_r.at[0])
+    b_lift[level] = jnp.sum(b_recv[...].astype(F32), axis=0).astype(BF16)
+    each_level(lambda z: push(b_lift.at[level], b_lift.at[level], 1, above(z)))
+
     s_all = nt(hot[...], da).astype(BF16)
-    a_send[0:H] = nt(eT[...], da).astype(BF16)
+    a_send[0:H] = nt(eT, da).astype(BF16)
     a_send[H : 2 * H] = nn(tab[...], s_all[0:T]).astype(BF16)
     a_send[2 * H : 3 * H] = nn(hT, s_all[T:]).astype(BF16)
-    a_send[3 * H :] = dw2.astype(BF16)
-    k_send[...] = jnp.zeros_like(k_send)
-    k_send[0:1] = row_of(acc).astype(BF16)
-    k_send[1:2] = gain_n_row.astype(BF16)
-
-    spread(a_send, a_recv, 1)
-    a_recv[mine] = a_send[shard(mine)]
-
-    to_last = pltpu.make_async_remote_copy(
-        src_ref=k_send, dst_ref=k_recv.at[mine], send_sem=psem_s.at[2], recv_sem=psem_r.at[2],
-        device_id=member(last), device_id_type=MESH,
-    )
-
-    @pl.when(mine != last)
-    def _():
-        to_last.start()
+    a_send[3 * H : 4 * H] = nt(pT, db).astype(BF16)
+    a_send[4 * H :] = jnp.zeros((GAIN_ROWS, H), BF16)
+    a_send[4 * H : 4 * H + 1] = row_of(acc).astype(BF16)
+    a_send[4 * H + 1 : 4 * H + 2] = gain_n_row.astype(BF16)
+
+    wide = share + GAIN_ROWS
+    wide_rows = pl.ds(last * share, wide)
+    narrow = pl.ds(0, share)
+    is_last = mine == last
+
+    def push_edge(i):
+        @pl.when(i == last)
+        def _():
+            push(a_send.at[wide_rows], a_recv.at[mine], 2, member(i))
+
+        @pl.when(i != last)
+        def _():
+            push(a_send.at[shard(i)], a_recv.at[mine, narrow], 2, member(i))
+
+    each_member(push_edge)
+
+    @pl.when(is_last)
+    def _():
+        a_recv[mine] = a_send[wide_rows]
+
+    @pl.when(jnp.logical_not(is_last))
+    def _():
+        a_recv[mine, 0:share] = a_send[shard(mine)]
 
     w1b = w1[...].astype(BF16)
     dghost = nt(s_all[C:T], w1b[H : 2 * H])
@@ -323,85 +321,82 @@
     for copy in ghost_back:
         copy.start()
 
-    def edge_out(i, _):
-        cols = pl.ds(pl.multiple_of(i * EDGE_TILE, EDGE_TILE), EDGE_TILE)
-        dx = nn(w1b[0:H], daT[:, cols]).astype(BF16).astype(F32)
-        gedge[cols, :] = (gT[:, cols] + dx).T
-        return 0
-
-    lax.fori_loop(0, tiles // 2, edge_out, 0)
-
-    all_arrived(a_recv, 1, psem_r)
-    all_arrived(b_recv, 0, psem_r)
-    zbuf[level, 0:share] = jnp.sum(a_recv[...].astype(F32), axis=0).astype(BF16)
-
-    @pl.when(mine == last)
-    def _():
-        k_recv[mine] = k_send[...]
-        all_arrived(k_recv, 2, psem_r)
-        total = jnp.sum(k_recv[:, 0:16].astype(F32), axis=0).astype(BF16)
-        zbuf[level, share : 2 * share] = jnp.zeros((share, H), BF16)
-        zbuf[level, share : share + 16] = total
-
-    @pl.when(mine != last)
-    def _():
-        zbuf[level, share : 2 * share] = jnp.sum(b_recv[...].astype(F32), axis=0).astype(BF16)
-
-    def climb(r, _):
-        pltpu.make_async_remote_copy(
-            src_ref=zbuf.at[level], dst_ref=zbuf.at[level], send_sem=psem_s.at[3], recv_sem=psem_r.at[3],
-            device_id=above(lax.rem(level + r, depth)), device_id_type=MESH,
-        ).start()
-        return 0
-
-    lax.fori_loop(1, depth, climb, 0)
-
-    lax.fori_loop(tiles // 2, tiles, edge_out, 0)
-
-    all_arrived(zbuf, 3, psem_r)
-    agbuf[mine] = (jnp.sum(zbuf[...].astype(F32), axis=0) * factor).astype(BF16)
-
-    def share_out(r, _):
-        pltpu.make_async_remote_copy(
-            src_ref=agbuf.at[mine], dst_ref=agbuf.at[mine], send_sem=psem_s.at[4], recv_sem=psem_r.at[4],
-            device_id=member(lax.rem(mine + r, group)), device_id_type=MESH,
-        ).start()
-        return 0
-
-    lax.fori_loop(1, group, share_out, 0)
-
+    await_bytes(b_levels, psem_r.at[1])
+    b_all[mine] = (jnp.sum(b_lift[...].astype(F32), axis=0) * factor).astype(BF16)
+    each_member(lambda i: push(b_all.at[mine], b_all.at[mine], 3, member(i)))
+
+    dx = nn(w1b[0:H], da).astype(BF16).astype(F32)
+    half_e = E // 2
+    gedge[0:half_e] = (gT[:, 0:half_e] + dx[:, 0:half_e]).T
+
+    @pl.when(is_last)
+    def _():
+        await_bytes(a_recv.at[pl.ds(0, group - 1)], psem_r.at[2])
+        a_lift[level] = jnp.sum(a_recv[...].astype(F32), axis=0).astype(BF16)
+        each_level(lambda z: push(a_lift.at[level], a_lift.at[level], 4, above(z)))
+
+    @pl.when(jnp.logical_not(is_last))
+    def _():
+        await_bytes(a_recv.at[pl.ds(0, group - 1), narrow], psem_r.at[2])
+        a_lift[level, 0:share] = jnp.sum(a_recv[:, 0:share].astype(F32), axis=0).astype(BF16)
+        each_level(lambda z: push(a_lift.at[level, narrow], a_lift.at[level, narrow], 4, above(z)))
+
+    gedge[half_e:E] = (gT[:, half_e:E] + dx[:, half_e:E]).T
     own = nt(s_all[0:C], w1b[H : 2 * H]).astype(BF16).astype(F32)
     own = own + nt(s_all[T:], w1b[2 * H : 3 * H]).astype(BF16).astype(F32)
+    gnode[...] = node_T.T + own
+
+    @pl.when(is_last)
+    def _():
+        await_bytes(a_lift.at[pl.ds(0, depth - 1)], psem_r.at[4])
+        total = (jnp.sum(a_lift[...].astype(F32), axis=0) * factor).astype(BF16)
+        a_all[wide_rows] = total
+        each_member(lambda i: push(a_all.at[wide_rows], a_all.at[wide_rows], 5, member(i)))
+
+    @pl.when(jnp.logical_not(is_last))
+    def _():
+        await_bytes(a_lift.at[pl.ds(0, depth - 1), narrow], psem_r.at[4])
+        total = (jnp.sum(a_lift[:, 0:share].astype(F32), axis=0) * factor).astype(BF16)
+        a_all[shard(mine)] = total
+        each_member(lambda i: push(a_all.at[shard(mine)], a_all.at[shard(mine)], 5, member(i)))
+
     for copy in ghost_back:
         copy.wait_recv()
     back = jnp.concatenate([gb_recv[0], gb_recv[1], gb_recv[2], gb_recv[0]], axis=0)
-    gnode[...] = node_T.T + own + nn(hot_out, back)
-
-    all_arrived(agbuf, 4, psem_r)
-
-    def landed(start, stop, offset):
-        count = (stop - start) // share
-        part = agbuf[start // share : start // share + count, offset : offset + share]
-        return part.astype(F32).reshape(stop - start, H)
-
-    gw1[...] = landed(0, 3 * H, 0)
-    gw2[...] = landed(3 * H, 4 * H, 0)
-    gn1[...] = landed(0, 2 * H, share)
-    gn2[...] = landed(2 * H, 3 * H, share)
-    tail = agbuf[last, share : share + 16].astype(F32)
+    gnode[...] += nn(hot_out, back)
+
+    await_bytes(b_shares, psem_r.at[3])
+    gn1[...] = b_all[0 : 2 * H // share].astype(F32).reshape(2 * H, H)
+    gn2[...] = b_all[2 * H // share : 3 * H // share].astype(F32).reshape(H, H)
+
+    for copy in ghost_out + ghost_back:
+        copy.wait_send()
+    await_bytes(b_others, psem_s.at[0])
+    await_bytes(b_levels, psem_s.at[1])
+    await_bytes(b_shares, psem_s.at[3])
+
+    without_share = a_all.at[pl.ds(0, (group - 1) * share)]
+    without_gains = a_all.at[pl.ds(0, (group - 1) * share + GAIN_ROWS)]
+
+    @pl.when(is_last)
+    def _():
+        await_bytes(without_share, psem_s.at[2])
+        await_bytes(a_lift.at[pl.ds(0, depth - 1)], psem_s.at[4])
+        await_bytes(a_recv.at[pl.ds(0, group - 1)], psem_s.at[5])
+        await_bytes(without_share, psem_r.at[5])
+
+    @pl.when(jnp.logical_not(is_last))
+    def _():
+        await_bytes(without_gains, psem_s.at[2])
+        await_bytes(a_lift.at[pl.ds(0, depth - 1), narrow], psem_s.at[4])
+        await_bytes(a_recv.at[pl.ds(0, group - 1), narrow], psem_s.at[5])
+        await_bytes(without_gains, psem_r.at[5])
+
+    gw1[...] = a_all[0 : 3 * H].astype(F32)
+    gw2[...] = a_all[3 * H : 4 * H].astype(F32)
+    tail = a_all[4 * H : 4 * H + GAIN_ROWS].astype(F32)
     geg[...] = tail[0:1]
     gng[...] = tail[1:2]
-
-    for copy in ghost_out + ghost_back:
-        copy.wait_send()
-    all_arrived(b_recv, 0, psem_s)
-    all_arrived(a_recv, 1, psem_s)
-    all_arrived(zbuf, 3, psem_s)
-    all_arrived(agbuf, 4, psem_s)
-
-    @pl.when(mine != last)
-    def _():
-        to_last.wait_send()
 
 
 def deliver(*refs):
@@ -450,17 +445,16 @@
         out_specs=[vmem] * 8,
         scratch_shapes=landing + [
             dma((14,)),
-            pltpu.VMEM((T + C, E), BF16), pltpu.VMEM((H, T), BF16), pltpu.VMEM((H, E), BF16),
-            pltpu.VMEM((H, E), F32), pltpu.VMEM((H, E), BF16), pltpu.VMEM((H, E), F32), pltpu.VMEM((H, E), F32),
-            pltpu.VMEM((1, E), F32), pltpu.VMEM((H, E), BF16), pltpu.VMEM((H, E), F32),
+            pltpu.VMEM((T + C, E), BF16), pltpu.VMEM((H, T), BF16),
+            pltpu.VMEM((H, E), F32), pltpu.VMEM((H, E), F32), pltpu.VMEM((H, E), F32),
             pltpu.VMEM((3, GQ, H), BF16), pltpu.VMEM((3, GQ, H), BF16),
             pltpu.VMEM((3, GQ, H), BF16), pltpu.VMEM((3, GQ, H), BF16),
             dma((3,)), dma((3,)), dma((3,)), dma((3,)),
+            pltpu.VMEM((4 * H + GAIN_ROWS, H), BF16), pltpu.VMEM((group, share + GAIN_ROWS, H), BF16),
+            pltpu.VMEM((depth, share + GAIN_ROWS, H), BF16), pltpu.VMEM((4 * H + GAIN_ROWS, H), BF16),
             pltpu.VMEM((4 * H, H), BF16), pltpu.VMEM((group, share, H), BF16),
-            pltpu.VMEM((4 * H, H), BF16), pltpu.VMEM((group, share, H), BF16),
-            pltpu.VMEM((16, H), BF16), pltpu.VMEM((group, 16, H), BF16),
-            pltpu.VMEM((depth, 2 * share, H), BF16), pltpu.VMEM((group, 2 * share, H), BF16),
-            dma((5,)), dma((5,)),
+            pltpu.VMEM((depth, share, H), BF16), pltpu.VMEM((group, share, H), BF16),
+            dma((6,)), dma((6,)),
         ],
         compiler_params=pltpu.CompilerParams(
             collective_id=0, has_side_effects=True, vmem_limit_bytes=40 * 1024 * 1024

time: 46.1 us -> 46.5 us (level)
  no operation moved by 1% of the time
where the time goes in v3:
time: 46.5 us; the launch traced here: 46.4 us
  Pallas kernels  45.1 us (97%)
  between operations  1.29 us (3%)
    pallas_call x1, Pallas kernels, on_device(): pl.pallas_call(functools.partial(kernel, (peers, dps, plane, factor)), ou...  43.9 us
    pallas_call x1, Pallas kernels, on_device(): pl.pallas_call(deliver, out_shape=results, in_specs=[vmem] * 8, out_specs...  1.27 us

profile of v3, /device:TPU:1, one launch (start us, length us, event | category | flops | bytes accessed | tf_op | source)
XLA Modules:
  0.0 46.4 jit_solution(13914322421672807864)
XLA Ops:
  1.3 43.9 %shard_map.197 = (f32[512,128]{1,0:T(8,128)S(1)}, f32[2048,128]{1,0:T(8,128)S(1)}, f32[384,128]{1,0:T(8,128)S(1)}, f32[128,128]{1,0:T(8,128)S(1)}, f32[1,128]{1,...) custom-call(bf16[512,128]{1,0:T(8,128)(2,1)} %bitcast.12, ...), custom_call_target="tpu_custom_call" | custom-call | tf_op jit(solution)/shard_map/pallas_call | solution.py:441
  45.2 1.3 %shard_map.198 = (f32[512,128]{1,0:T(8,128)}, f32[2048,128]{1,0:T(8,128)}, f32[384,128]{1,0:T(8,128)}, f32[128,128]{1,0:T(8,128)}, f32[1,128]{1,0:T(1,128)}, /*i...) custom-call(f32[512,128]{1,0:T(8,128)S(1)} %get-tuple-element.24.refs_0_, ...), custom_call_target="tpu_custom_call" | custom-call | tf_op jit(solution)/shard_map/pallas_call | solution.py:464

commit v4 on v3

--- a/solution.py
+++ b/solution.py
@@ -71,7 +71,7 @@
     eg_hbm, ng_hbm, n1_hbm, n2_hbm, cotn_hbm, cote_hbm,
     gnode, gedge, gw1, gw2, geg, gn1, gn2, gng,
     h_v, rows, e_v, snd, rcv, w1, w2, cnt, eg, ng, n1, n2, cn_v, ce_v, in_sem,
-    hot, tab, dsil, nhat, gT,
+    hot, xT, ceT, dsil, nhat, gT,
     gs_send, gs_recv, gb_send, gb_recv, gsem_s, gsem_r, bsem_s, bsem_r,
     a_send, a_recv, a_lift, a_all, b_send, b_recv, b_lift, b_all, psem_s, psem_r,
 ):
@@ -102,6 +102,28 @@
     def above(z):
         return (z * plane + m % plane, core)
 
+    barrier = pltpu.get_barrier_semaphore()
+
+    def greet(to):
+        pl.semaphore_signal(barrier, inc=1, device_id=to, device_id_type=MESH)
+
+    def each_member(act):
+        def go(r, _):
+            act(lax.rem(mine + r, group))
+            return 0
+
+        lax.fori_loop(1, group, go, 0)
+
+    def each_level(act):
+        def go(r, _):
+            act(lax.rem(level + r, depth))
+            return 0
+
+        lax.fori_loop(1, depth, go, 0)
+
+    greet((partner, core))
+    greet((left, core))
+    greet((right, core))
     sources = (
         node_hbm, rows_hbm, edge_hbm, snd_hbm, rcv_hbm, w1_hbm, w2_hbm, cnt_hbm,
         eg_hbm, ng_hbm, n1_hbm, n2_hbm, cotn_hbm, cote_hbm,
@@ -113,21 +135,8 @@
     for load in loads:
         load.start()
 
-    barrier = pltpu.get_barrier_semaphore()
-
-    def greet(r, _):
-        pl.semaphore_signal(barrier, inc=1, device_id=member(lax.rem(mine + r, group)), device_id_type=MESH)
-        return 0
-
-    lax.fori_loop(1, group, greet, 0)
-
-    def greet_above(r, _):
-        pl.semaphore_signal(barrier, inc=1, device_id=above(lax.rem(level + r, depth)), device_id_type=MESH)
-        return 0
-
-    lax.fori_loop(1, depth, greet_above, 0)
-    for side in (left, right):
-        pl.semaphore_signal(barrier, inc=1, device_id=(side, core), device_id_type=MESH)
+    each_level(lambda z: greet(above(z)))
+    each_member(lambda i: greet(member(i)))
 
     eye_r = lax.broadcasted_iota(jnp.int32, (H, H), 0)
     eye_c = lax.broadcasted_iota(jnp.int32, (H, H), 1)
@@ -143,13 +152,12 @@
     hot_out = one_hot(jnp.where(used, rows[...], -1), C)
 
     hT = nt(eye, h_v[...]).astype(BF16)
-    tab[:, 0:C] = hT
     picked = nn(hT, hot_out).T
     gs_send[0] = (picked[0:GQ] + picked[3 * GQ : 4 * GQ]).astype(BF16)
     gs_send[1] = picked[GQ : 2 * GQ].astype(BF16)
     gs_send[2] = picked[2 * GQ : 3 * GQ].astype(BF16)
 
-    pl.semaphore_wait(barrier, (group - 1) + (depth - 1) + 2)
+    pl.semaphore_wait(barrier, (group - 1) + (depth - 1) + 3)
 
     ghost_out = [
         pltpu.make_async_remote_copy(
@@ -175,9 +183,21 @@
     xs = nn(hT, hot_s[0:C]).astype(BF16)
     xr = nn(hT, hot_r).astype(BF16)
     a0 = nn(w1T, jnp.concatenate([eT, xs, xr], axis=0))
-
-    for load in loads[7:12]:
+    xT[0:H] = eT
+    xT[H : 2 * H] = xs
+    xT[2 * H : 3 * H] = xr
+
+    for load in loads[7:]:
         load.wait()
+    ceT[...] = nt(eye, ce_v[...]).astype(BF16)
+    cnT = nt(eye, cn_v[...])
+    n1b = n1[...].astype(BF16)
+    n2b = n2[...].astype(BF16)
+    n1T = nt(eye, n1b).astype(BF16)
+    n2T = nt(eye, n2b).astype(BF16)
+    w1b = w1[...].astype(BF16)
+    w2b = w2[...].astype(BF16)
+    slot = lax.broadcasted_iota(jnp.int32, (1, E), 1)
     gain_e = column_of(eg[...])
     gain_n = column_of(ng[...])
     gain_tile = across(gain_e, E)
@@ -190,13 +210,12 @@
     last_here = jnp.logical_and(lane >= 3 * GQ, jnp.logical_not(low))
     here = jnp.logical_or(middle, jnp.logical_or(first_here, last_here))
     ghost_T = jnp.where(here, nt(eye, ghosts), 0.0).astype(BF16)
-    tab[:, C:T] = ghost_T
-
-    slot = lax.broadcasted_iota(jnp.int32, (1, E), 1)
+
     live = jnp.where(slot < count, 1.0, 0.0)
 
     xg = nn(ghost_T, hot[C:T]).astype(BF16)
     p, d = silu_parts(a0 + nn(w1s_T, xg))
+    xT[H : 2 * H] += xg
     pT = p.astype(BF16)
     dsil[...] = d
     nh, e_rs = normed(nn(w2T, pT))
@@ -204,16 +223,10 @@
     msg = (live * (eT.astype(F32) + live * (nh * gain_tile))).astype(BF16)
     agg = nt(msg, hot[T : T + C]).astype(BF16)
 
-    n1b = n1[...].astype(BF16)
-    n2b = n2[...].astype(BF16)
-    n1T = nt(eye, n1b).astype(BF16)
-    n2T = nt(eye, n2b).astype(BF16)
-    loads[12].wait()
     yT = jnp.concatenate([hT, agg], axis=0)
     r, dr_ = silu_parts(nn(n1T, yT))
     r = r.astype(BF16)
     nh, rs = normed(nn(n2T, r))
-    cnT = nt(eye, cn_v[...])
     acc = folded(cnT * nh)
     ds = normed_back(cnT * across(gain_n, C), nh, rs).astype(BF16)
     dc = (nn(n2b, ds).astype(BF16).astype(F32) * dr_).astype(BF16)
@@ -237,20 +250,6 @@
     def await_bytes(ref, sem):
         pltpu.make_async_copy(ref, ref, sem).wait()
 
-    def each_member(act):
-        def go(r, _):
-            act(lax.rem(mine + r, group))
-            return 0
-
-        lax.fori_loop(1, group, go, 0)
-
-    def each_level(act):
-        def go(r, _):
-            act(lax.rem(level + r, depth))
-            return 0
-
-        lax.fori_loop(1, depth, go, 0)
-
     b_others = b_recv.at[pl.ds(0, group - 1)]
     b_levels = b_lift.at[pl.ds(0, depth - 1)]
     b_shares = b_all.at[pl.ds(0, group - 1)]
@@ -258,9 +257,7 @@
     each_member(lambda i: push(b_send.at[shard(i)], b_recv.at[mine], 0, member(i)))
     b_recv[mine] = b_send[shard(mine)]
 
-    loads[13].wait()
-    w2b = w2[...].astype(BF16)
-    g = nt(eye, ce_v[...]) + live * nn(dagg, hot[T : T + C])
+    g = ceT[...].astype(F32) + live * nn(dagg, hot[T : T + C])
     gT[...] = g
     dd = live * g
     nh = nhat[...]
@@ -269,18 +266,11 @@
     dp = nn(w2b, db).astype(BF16).astype(F32)
     da = (dp * dsil[...]).astype(BF16)
 
-    await_bytes(b_others, psem_r.at[0])
-    b_lift[level] = jnp.sum(b_recv[...].astype(F32), axis=0).astype(BF16)
-    each_level(lambda z: push(b_lift.at[level], b_lift.at[level], 1, above(z)))
-
-    s_all = nt(hot[...], da).astype(BF16)
-    a_send[0:H] = nt(eT, da).astype(BF16)
-    a_send[H : 2 * H] = nn(tab[...], s_all[0:T]).astype(BF16)
-    a_send[2 * H : 3 * H] = nn(hT, s_all[T:]).astype(BF16)
+    a_send[0 : 3 * H] = nt(xT[...], da).astype(BF16)
     a_send[3 * H : 4 * H] = nt(pT, db).astype(BF16)
-    a_send[4 * H :] = jnp.zeros((GAIN_ROWS, H), BF16)
-    a_send[4 * H : 4 * H + 1] = row_of(acc).astype(BF16)
-    a_send[4 * H + 1 : 4 * H + 2] = gain_n_row.astype(BF16)
+    gain_row = lax.broadcasted_iota(jnp.int32, (GAIN_ROWS, H), 0)
+    gains = jnp.where(gain_row == 0, row_of(acc), jnp.where(gain_row == 1, gain_n_row, 0.0))
+    a_send[4 * H :] = gains.astype(BF16)
 
     wide = share + GAIN_ROWS
     wide_rows = pl.ds(last * share, wide)
@@ -306,7 +296,7 @@
     def _():
         a_recv[mine, 0:share] = a_send[shard(mine)]
 
-    w1b = w1[...].astype(BF16)
+    s_all = nt(hot[...], da).astype(BF16)
     dghost = nt(s_all[C:T], w1b[H : 2 * H])
     gb_send[0] = (dghost[0:GQ] + dghost[3 * GQ : 4 * GQ]).astype(BF16)
     gb_send[1] = dghost[GQ : 2 * GQ].astype(BF16)
@@ -321,25 +311,29 @@
     for copy in ghost_back:
         copy.start()
 
+    await_bytes(b_others, psem_r.at[0])
+    b_lift[level] = jnp.sum(b_recv[...].astype(F32), axis=0).astype(BF16)
+    each_level(lambda z: push(b_lift.at[level], b_lift.at[level], 1, above(z)))
+
+    dx = nn(w1b[0:H], da).astype(BF16).astype(F32)
+    half_e = E // 2
+    gedge[0:half_e] = (gT[:, 0:half_e] + dx[:, 0:half_e]).T
+
+    @pl.when(is_last)
+    def _():
+        await_bytes(a_recv.at[pl.ds(0, group - 1)], psem_r.at[2])
+        a_lift[level] = jnp.sum(a_recv[...].astype(F32), axis=0).astype(BF16)
+        each_level(lambda z: push(a_lift.at[level], a_lift.at[level], 4, above(z)))
+
+    @pl.when(jnp.logical_not(is_last))
+    def _():
+        await_bytes(a_recv.at[pl.ds(0, group - 1), narrow], psem_r.at[2])
+        a_lift[level, 0:share] = jnp.sum(a_recv[:, 0:share].astype(F32), axis=0).astype(BF16)
+        each_level(lambda z: push(a_lift.at[level, narrow], a_lift.at[level, narrow], 4, above(z)))
+
     await_bytes(b_levels, psem_r.at[1])
     b_all[mine] = (jnp.sum(b_lift[...].astype(F32), axis=0) * factor).astype(BF16)
     each_member(lambda i: push(b_all.at[mine], b_all.at[mine], 3, member(i)))
-
-    dx = nn(w1b[0:H], da).astype(BF16).astype(F32)
-    half_e = E // 2
-    gedge[0:half_e] = (gT[:, 0:half_e] + dx[:, 0:half_e]).T
-
-    @pl.when(is_last)
-    def _():
-        await_bytes(a_recv.at[pl.ds(0, group - 1)], psem_r.at[2])
-        a_lift[level] = jnp.sum(a_recv[...].astype(F32), axis=0).astype(BF16)
-        each_level(lambda z: push(a_lift.at[level], a_lift.at[level], 4, above(z)))
-
-    @pl.when(jnp.logical_not(is_last))
-    def _():
-        await_bytes(a_recv.at[pl.ds(0, group - 1), narrow], psem_r.at[2])
-        a_lift[level, 0:share] = jnp.sum(a_recv[:, 0:share].astype(F32), axis=0).astype(BF16)
-        each_level(lambda z: push(a_lift.at[level, narrow], a_lift.at[level, narrow], 4, above(z)))
 
     gedge[half_e:E] = (gT[:, half_e:E] + dx[:, half_e:E]).T
     own = nt(s_all[0:C], w1b[H : 2 * H]).astype(BF16).astype(F32)
@@ -445,7 +439,7 @@
         out_specs=[vmem] * 8,
         scratch_shapes=landing + [
             dma((14,)),
-            pltpu.VMEM((T + C, E), BF16), pltpu.VMEM((H, T), BF16),
+            pltpu.VMEM((T + C, E), BF16), pltpu.VMEM((3 * H, E), BF16), pltpu.VMEM((H, E), BF16),
             pltpu.VMEM((H, E), F32), pltpu.VMEM((H, E), F32), pltpu.VMEM((H, E), F32),
             pltpu.VMEM((3, GQ, H), BF16), pltpu.VMEM((3, GQ, H), BF16),
             pltpu.VMEM((3, GQ, H), BF16), pltpu.VMEM((3, GQ, H), BF16),

time: 46.5 us -> 40.1 us (0.86)
  Pallas kernels: 45.1 us -> 38.7 us
    pallas_call x1, Pallas kernels: 43.9 us -> 37.4 us  [on_device(): pl.pallas_call(functools.partial(kernel, (peers, dps, plane, factor)), ou...]
where the time goes in v4:
time: 40.1 us; the launch traced here: 40 us
  Pallas kernels  38.7 us (97%)
  between operations  1.29 us (3%)
    pallas_call x1, Pallas kernels, on_device(): pl.pallas_call(functools.partial(kernel, (peers, dps, plane, factor)), ou...  37.4 us
    pallas_call x1, Pallas kernels, on_device(): pl.pallas_call(deliver, out_shape=results, in_specs=[vmem] * 8, out_specs...  1.27 us

profile of v4, /device:TPU:1, one launch (start us, length us, event | category | flops | bytes accessed | tf_op | source)
XLA Modules:
  0.0 40.0 jit_solution(3518790720094078750)
XLA Ops:
  1.3 37.4 %shard_map.197 = (f32[512,128]{1,0:T(8,128)S(1)}, f32[2048,128]{1,0:T(8,128)S(1)}, f32[384,128]{1,0:T(8,128)S(1)}, f32[128,128]{1,0:T(8,128)S(1)}, f32[1,128]{1,...) custom-call(bf16[512,128]{1,0:T(8,128)(2,1)} %bitcast.12, ...), custom_call_target="tpu_custom_call" | custom-call | tf_op jit(solution)/shard_map/pallas_call | solution.py:435
  38.7 1.3 %shard_map.198 = (f32[512,128]{1,0:T(8,128)}, f32[2048,128]{1,0:T(8,128)}, f32[384,128]{1,0:T(8,128)}, f32[128,128]{1,0:T(8,128)}, f32[1,128]{1,0:T(1,128)}, /*i...) custom-call(f32[512,128]{1,0:T(8,128)S(1)} %get-tuple-element.24.refs_0_, ...), custom_call_target="tpu_custom_call" | custom-call | tf_op jit(solution)/shard_map/pallas_call | solution.py:458

commit v5 on v4

--- a/solution.py
+++ b/solution.py
@@ -11,6 +11,19 @@
 F32 = jnp.float32
 BF16 = jnp.bfloat16
 GAIN_ROWS = 16
+
+
+SIDE = 4
+PIECES = 4
+
+
+def ring(offset, size):
+    return min(offset, size - offset)
+
+
+def farthest_first(plane, dps):
+    steps = [(ox, oy, oc) for ox in range(plane // SIDE) for oy in range(SIDE) for oc in range(dps)]
+    return sorted(steps[1:], key=lambda o: -(ring(o[0], SIDE) + ring(o[1], SIDE)))
 
 
 def nn(a, b):
@@ -99,6 +112,9 @@
     def member(i):
         return (level * plane + i // dps, i % dps)
 
+    mx = (m % plane) // SIDE
+    my = m % SIDE
+
     def above(z):
         return (z * plane + m % plane, core)
 
@@ -108,18 +124,14 @@
         pl.semaphore_signal(barrier, inc=1, device_id=to, device_id_type=MESH)
 
     def each_member(act):
-        def go(r, _):
-            act(lax.rem(mine + r, group))
-            return 0
-
-        lax.fori_loop(1, group, go, 0)
+        for ox, oy, oc in farthest_first(plane, dps):
+            column = lax.rem(mx + ox, SIDE) * SIDE + lax.rem(my + oy, SIDE)
+            other = lax.rem(core + oc, dps)
+            act(column * dps + other, (level * plane + column, other))
 
     def each_level(act):
-        def go(r, _):
-            act(lax.rem(level + r, depth))
-            return 0
-
-        lax.fori_loop(1, depth, go, 0)
+        for o in sorted(range(1, depth), key=lambda o: -ring(o, depth)):
+            act(above(lax.rem(level + o, depth)))
 
     greet((partner, core))
     greet((left, core))
@@ -135,8 +147,8 @@
     for load in loads:
         load.start()
 
-    each_level(lambda z: greet(above(z)))
-    each_member(lambda i: greet(member(i)))
+    each_level(greet)
+    each_member(lambda i, to: greet(to))
 
     eye_r = lax.broadcasted_iota(jnp.int32, (H, H), 0)
     eye_c = lax.broadcasted_iota(jnp.int32, (H, H), 1)
@@ -254,7 +266,7 @@
     b_levels = b_lift.at[pl.ds(0, depth - 1)]
     b_shares = b_all.at[pl.ds(0, group - 1)]
 
-    each_member(lambda i: push(b_send.at[shard(i)], b_recv.at[mine], 0, member(i)))
+    each_member(lambda i, to: push(b_send.at[shard(i)], b_recv.at[mine], 0, to))
     b_recv[mine] = b_send[shard(mine)]
 
     g = ceT[...].astype(F32) + live * nn(dagg, hot[T : T + C])
@@ -277,16 +289,12 @@
     narrow = pl.ds(0, share)
     is_last = mine == last
 
-    def push_edge(i):
-        @pl.when(i == last)
-        def _():
-            push(a_send.at[wide_rows], a_recv.at[mine], 2, member(i))
-
-        @pl.when(i != last)
-        def _():
-            push(a_send.at[shard(i)], a_recv.at[mine, narrow], 2, member(i))
-
-    each_member(push_edge)
+    gain_rows = pl.ds(group * share, GAIN_ROWS)
+    each_member(lambda i, to: push(a_send.at[shard(i)], a_recv.at[mine, narrow], 2, to))
+
+    @pl.when(jnp.logical_not(is_last))
+    def _():
+        push(a_send.at[gain_rows], a_recv.at[mine, pl.ds(share, GAIN_ROWS)], 2, member(last))
 
     @pl.when(is_last)
     def _():
@@ -313,7 +321,7 @@
 
     await_bytes(b_others, psem_r.at[0])
     b_lift[level] = jnp.sum(b_recv[...].astype(F32), axis=0).astype(BF16)
-    each_level(lambda z: push(b_lift.at[level], b_lift.at[level], 1, above(z)))
+    each_level(lambda to: push(b_lift.at[level], b_lift.at[level], 1, to))
 
     dx = nn(w1b[0:H], da).astype(BF16).astype(F32)
     half_e = E // 2
@@ -323,17 +331,17 @@
     def _():
         await_bytes(a_recv.at[pl.ds(0, group - 1)], psem_r.at[2])
         a_lift[level] = jnp.sum(a_recv[...].astype(F32), axis=0).astype(BF16)
-        each_level(lambda z: push(a_lift.at[level], a_lift.at[level], 4, above(z)))
+        each_level(lambda to: push(a_lift.at[level], a_lift.at[level], 4, to))
 
     @pl.when(jnp.logical_not(is_last))
     def _():
         await_bytes(a_recv.at[pl.ds(0, group - 1), narrow], psem_r.at[2])
         a_lift[level, 0:share] = jnp.sum(a_recv[:, 0:share].astype(F32), axis=0).astype(BF16)
-        each_level(lambda z: push(a_lift.at[level, narrow], a_lift.at[level, narrow], 4, above(z)))
+        each_level(lambda to: push(a_lift.at[level, narrow], a_lift.at[level, narrow], 4, to))
 
     await_bytes(b_levels, psem_r.at[1])
     b_all[mine] = (jnp.sum(b_lift[...].astype(F32), axis=0) * factor).astype(BF16)
-    each_member(lambda i: push(b_all.at[mine], b_all.at[mine], 3, member(i)))
+    each_member(lambda i, to: push(b_all.at[mine], b_all.at[mine], 3, to))
 
     gedge[half_e:E] = (gT[:, half_e:E] + dx[:, half_e:E]).T
     own = nt(s_all[0:C], w1b[H : 2 * H]).astype(BF16).astype(F32)
@@ -345,14 +353,14 @@
         await_bytes(a_lift.at[pl.ds(0, depth - 1)], psem_r.at[4])
         total = (jnp.sum(a_lift[...].astype(F32), axis=0) * factor).astype(BF16)
         a_all[wide_rows] = total
-        each_member(lambda i: push(a_all.at[wide_rows], a_all.at[wide_rows], 5, member(i)))
+        each_member(lambda i, to: push(a_all.at[wide_rows], a_all.at[wide_rows], 5, to))
 
     @pl.when(jnp.logical_not(is_last))
     def _():
         await_bytes(a_lift.at[pl.ds(0, depth - 1), narrow], psem_r.at[4])
         total = (jnp.sum(a_lift[:, 0:share].astype(F32), axis=0) * factor).astype(BF16)
         a_all[shard(mine)] = total
-        each_member(lambda i: push(a_all.at[shard(mine)], a_all.at[shard(mine)], 5, member(i)))
+        each_member(lambda i, to: push(a_all.at[shard(mine)], a_all.at[shard(mine)], 5, to))
 
     for copy in ghost_back:
         copy.wait_recv()
@@ -396,7 +404,16 @@
 def deliver(*refs):
     n = len(refs) // 2
     sem = refs[-1]
-    copies = [pltpu.make_async_copy(refs[i], refs[n + i], sem.at[i]) for i in range(n)]
+    pairs = []
+    for i in range(n):
+        src, dst = refs[i], refs[n + i]
+        size = src.shape[0]
+        if size > 512:
+            cuts = [pl.ds(j * size // PIECES, size // PIECES) for j in range(PIECES)]
+            pairs += [(src.at[c], dst.at[c]) for c in cuts]
+        else:
+            pairs.append((src, dst))
+    copies = [pltpu.make_async_copy(src, dst, sem.at[i]) for i, (src, dst) in enumerate(pairs)]
     for copy in copies:
         copy.start()
     for copy in copies:
@@ -460,7 +477,7 @@
         out_shape=results,
         in_specs=[vmem] * 8,
         out_specs=[hbm] * 8,
-        scratch_shapes=[dma((8,))],
+        scratch_shapes=[dma((7 + PIECES,))],
     )(*outs)
     return (
         outs[0][None], outs[1][None], outs[2], outs[3], outs[4].reshape(H), outs[5], outs[6], outs[7].reshape(H)

time: 40.1 us -> 38.5 us (0.960)
  Pallas kernels: 38.7 us -> 37.1 us
    pallas_call x1, Pallas kernels: 37.4 us -> 35.8 us  [on_device(): pl.pallas_call(functools.partial(kernel, (peers, dps, plane, factor)), ou...]
where the time goes in v5:
time: 38.5 us; the launch traced here: 38.4 us
  Pallas kernels  37.1 us (96%)
  between operations  1.29 us (3%)
    pallas_call x1, Pallas kernels, on_device(): pl.pallas_call(functools.partial(kernel, (peers, dps, plane, factor)), ou...  35.8 us
    pallas_call x1, Pallas kernels, on_device(): pl.pallas_call(deliver, out_shape=results, in_specs=[vmem] * 8, out_specs...  1.3 us

profile of v5, /device:TPU:1, one launch (start us, length us, event | category | flops | bytes accessed | tf_op | source)
XLA Modules:
  0.0 38.4 jit_solution(6587537393328119546)
XLA Ops:
  1.3 35.8 %shard_map.197 = (f32[512,128]{1,0:T(8,128)S(1)}, f32[2048,128]{1,0:T(8,128)S(1)}, f32[384,128]{1,0:T(8,128)S(1)}, f32[128,128]{1,0:T(8,128)S(1)}, f32[1,128]{1,...) custom-call(bf16[512,128]{1,0:T(8,128)(2,1)} %bitcast.12, ...), custom_call_target="tpu_custom_call" | custom-call | tf_op jit(solution)/shard_map/pallas_call | solution.py:452
  37.1 1.3 %shard_map.198 = (f32[512,128]{1,0:T(8,128)}, f32[2048,128]{1,0:T(8,128)}, f32[384,128]{1,0:T(8,128)}, f32[128,128]{1,0:T(8,128)}, f32[1,128]{1,0:T(1,128)}, /*i...) custom-call(f32[512,128]{1,0:T(8,128)S(1)} %get-tuple-element.24.refs_0_, ...), custom_call_target="tpu_custom_call" | custom-call | tf_op jit(solution)/shard_map/pallas_call | solution.py:475

commit v6 on v5

--- a/solution.py
+++ b/solution.py
@@ -84,7 +84,7 @@
     eg_hbm, ng_hbm, n1_hbm, n2_hbm, cotn_hbm, cote_hbm,
     gnode, gedge, gw1, gw2, geg, gn1, gn2, gng,
     h_v, rows, e_v, snd, rcv, w1, w2, cnt, eg, ng, n1, n2, cn_v, ce_v, in_sem,
-    hot, xT, ceT, dsil, nhat, gT,
+    hot, xT, ceT, live_eT, live_gain, dsil, nhat, gT,
     gs_send, gs_recv, gb_send, gb_recv, gsem_s, gsem_r, bsem_s, bsem_r,
     a_send, a_recv, a_lift, a_all, b_send, b_recv, b_lift, b_all, psem_s, psem_r,
 ):
@@ -134,8 +134,6 @@
             act(above(lax.rem(level + o, depth)))
 
     greet((partner, core))
-    greet((left, core))
-    greet((right, core))
     sources = (
         node_hbm, rows_hbm, edge_hbm, snd_hbm, rcv_hbm, w1_hbm, w2_hbm, cnt_hbm,
         eg_hbm, ng_hbm, n1_hbm, n2_hbm, cotn_hbm, cote_hbm,
@@ -144,7 +142,11 @@
     loads = [
         pltpu.make_async_copy(src, dst, in_sem.at[i]) for i, (src, dst) in enumerate(zip(sources, places))
     ]
-    for load in loads:
+    loads[0].start()
+    loads[1].start()
+    greet((left, core))
+    greet((right, core))
+    for load in loads[2:]:
         load.start()
 
     each_level(greet)
@@ -196,7 +198,6 @@
     xr = nn(hT, hot_r).astype(BF16)
     a0 = nn(w1T, jnp.concatenate([eT, xs, xr], axis=0))
     xT[0:H] = eT
-    xT[H : 2 * H] = xs
     xT[2 * H : 3 * H] = xr
 
     for load in loads[7:]:
@@ -215,6 +216,10 @@
     gain_tile = across(gain_e, E)
     count = cnt[0, 0]
 
+    live = jnp.where(slot < count, 1.0, 0.0)
+    live_eT[...] = live * eT.astype(F32)
+    live_gain[...] = live * gain_tile
+
     for copy in ghost_out:
         copy.wait_recv()
     ghosts = jnp.concatenate([gs_recv[0], gs_recv[1], gs_recv[2], gs_recv[0]], axis=0)
@@ -223,16 +228,14 @@
     here = jnp.logical_or(middle, jnp.logical_or(first_here, last_here))
     ghost_T = jnp.where(here, nt(eye, ghosts), 0.0).astype(BF16)
 
-    live = jnp.where(slot < count, 1.0, 0.0)
-
-    xg = nn(ghost_T, hot[C:T]).astype(BF16)
-    p, d = silu_parts(a0 + nn(w1s_T, xg))
-    xT[H : 2 * H] += xg
+    xg = nn(ghost_T, hot[C:T])
+    p, d = silu_parts(a0 + nn(w1s_T, xg.astype(BF16)))
+    xT[H : 2 * H] = (xs.astype(F32) + xg).astype(BF16)
     pT = p.astype(BF16)
     dsil[...] = d
     nh, e_rs = normed(nn(w2T, pT))
     nhat[...] = nh
-    msg = (live * (eT.astype(F32) + live * (nh * gain_tile))).astype(BF16)
+    msg = (live_eT[...] + live_gain[...] * nh).astype(BF16)
     agg = nt(msg, hot[T : T + C]).astype(BF16)
 
     yT = jnp.concatenate([hT, agg], axis=0)
@@ -274,11 +277,11 @@
     dd = live * g
     nh = nhat[...]
     acc = folded(dd * nh)
-    db = normed_back(dd * gain_tile, nh, e_rs).astype(BF16)
+    db = normed_back(live_gain[...] * g, nh, e_rs).astype(BF16)
     dp = nn(w2b, db).astype(BF16).astype(F32)
     da = (dp * dsil[...]).astype(BF16)
 
-    a_send[0 : 3 * H] = nt(xT[...], da).astype(BF16)
+    a_send[0 : 3 * H] = nt(da, xT[...]).T.astype(BF16)
     a_send[3 * H : 4 * H] = nt(pT, db).astype(BF16)
     gain_row = lax.broadcasted_iota(jnp.int32, (GAIN_ROWS, H), 0)
     gains = jnp.where(gain_row == 0, row_of(acc), jnp.where(gain_row == 1, gain_n_row, 0.0))
@@ -304,8 +307,8 @@
     def _():
         a_recv[mine, 0:share] = a_send[shard(mine)]
 
-    s_all = nt(hot[...], da).astype(BF16)
-    dghost = nt(s_all[C:T], w1b[H : 2 * H])
+    s_T = nt(da, hot[...]).astype(BF16)
+    dghost = nn(w1b[H : 2 * H], s_T[:, C:T]).T
     gb_send[0] = (dghost[0:GQ] + dghost[3 * GQ : 4 * GQ]).astype(BF16)
     gb_send[1] = dghost[GQ : 2 * GQ].astype(BF16)
     gb_send[2] = dghost[2 * GQ : 3 * GQ].astype(BF16)
@@ -344,9 +347,8 @@
     each_member(lambda i, to: push(b_all.at[mine], b_all.at[mine], 3, to))
 
     gedge[half_e:E] = (gT[:, half_e:E] + dx[:, half_e:E]).T
-    own = nt(s_all[0:C], w1b[H : 2 * H]).astype(BF16).astype(F32)
-    own = own + nt(s_all[T:], w1b[2 * H : 3 * H]).astype(BF16).astype(F32)
-    gnode[...] = node_T.T + own
+    own = nn(w1b[H : 2 * H], s_T[:, 0:C]) + nn(w1b[2 * H : 3 * H], s_T[:, T:])
+    gnode[...] = (node_T + own).T
 
     @pl.when(is_last)
     def _():
@@ -457,6 +459,7 @@
         scratch_shapes=landing + [
             dma((14,)),
             pltpu.VMEM((T + C, E), BF16), pltpu.VMEM((3 * H, E), BF16), pltpu.VMEM((H, E), BF16),
+            pltpu.VMEM((H, E), F32), pltpu.VMEM((H, E), F32),
             pltpu.VMEM((H, E), F32), pltpu.VMEM((H, E), F32), pltpu.VMEM((H, E), F32),
             pltpu.VMEM((3, GQ, H), BF16), pltpu.VMEM((3, GQ, H), BF16),
             pltpu.VMEM((3, GQ, H), BF16), pltpu.VMEM((3, GQ, H), BF16),

time: 38.5 us -> 38.1 us (0.990)
  Pallas kernels: 37.1 us -> 36.7 us
    pallas_call x1, Pallas kernels: 35.8 us -> 35.4 us  [on_device(): pl.pallas_call(functools.partial(kernel, (peers, dps, plane, factor)), ou...]
where the time goes in v6:
time: 38.1 us; the launch traced here: 38 us
  Pallas kernels  36.7 us (96%)
  between operations  1.29 us (3%)
    pallas_call x1, Pallas kernels, on_device(): pl.pallas_call(functools.partial(kernel, (peers, dps, plane, factor)), ou...  35.4 us
    pallas_call x1, Pallas kernels, on_device(): pl.pallas_call(deliver, out_shape=results, in_specs=[vmem] * 8, out_specs...  1.3 us

profile of v6, /device:TPU:1, one launch (start us, length us, event | category | flops | bytes accessed | tf_op | source)
XLA Modules:
  0.0 38.0 jit_solution(11796948425061120518)
XLA Ops:
  1.3 35.4 %shard_map.197 = (f32[512,128]{1,0:T(8,128)S(1)}, f32[2048,128]{1,0:T(8,128)S(1)}, f32[384,128]{1,0:T(8,128)S(1)}, f32[128,128]{1,0:T(8,128)S(1)}, f32[1,128]{1,...) custom-call(bf16[512,128]{1,0:T(8,128)(2,1)} %bitcast.12, ...), custom_call_target="tpu_custom_call" | custom-call | tf_op jit(solution)/shard_map/pallas_call | solution.py:454
  36.7 1.3 %shard_map.198 = (f32[512,128]{1,0:T(8,128)}, f32[2048,128]{1,0:T(8,128)}, f32[384,128]{1,0:T(8,128)}, f32[128,128]{1,0:T(8,128)}, f32[1,128]{1,0:T(1,128)}, /*i...) custom-call(f32[512,128]{1,0:T(8,128)S(1)} %get-tuple-element.24.refs_0_, ...), custom_call_target="tpu_custom_call" | custom-call | tf_op jit(solution)/shard_map/pallas_call | solution.py:478

commit v7 on v6

--- a/solution.py
+++ b/solution.py
@@ -149,7 +149,9 @@
     for load in loads[2:]:
         load.start()
 
-    each_level(greet)
+    for o in range(1, depth):
+        if o != depth // 2:
+            greet(above(lax.rem(level + o, depth)))
     each_member(lambda i, to: greet(to))
 
     eye_r = lax.broadcasted_iota(jnp.int32, (H, H), 0)
@@ -171,7 +173,7 @@
     gs_send[1] = picked[GQ : 2 * GQ].astype(BF16)
     gs_send[2] = picked[2 * GQ : 3 * GQ].astype(BF16)
 
-    pl.semaphore_wait(barrier, (group - 1) + (depth - 1) + 3)
+    pl.semaphore_wait(barrier, (group - 1) + (depth - 2) + 3)
 
     ghost_out = [
         pltpu.make_async_remote_copy(
@@ -326,21 +328,21 @@
     b_lift[level] = jnp.sum(b_recv[...].astype(F32), axis=0).astype(BF16)
     each_level(lambda to: push(b_lift.at[level], b_lift.at[level], 1, to))
 
+    @pl.when(is_last)
+    def _():
+        await_bytes(a_recv.at[pl.ds(0, group - 1)], psem_r.at[2])
+        a_lift[level] = jnp.sum(a_recv[...].astype(F32), axis=0).astype(BF16)
+        each_level(lambda to: push(a_lift.at[level], a_lift.at[level], 4, to))
+
+    @pl.when(jnp.logical_not(is_last))
+    def _():
+        await_bytes(a_recv.at[pl.ds(0, group - 1), narrow], psem_r.at[2])
+        a_lift[level, 0:share] = jnp.sum(a_recv[:, 0:share].astype(F32), axis=0).astype(BF16)
+        each_level(lambda to: push(a_lift.at[level, narrow], a_lift.at[level, narrow], 4, to))
+
     dx = nn(w1b[0:H], da).astype(BF16).astype(F32)
     half_e = E // 2
     gedge[0:half_e] = (gT[:, 0:half_e] + dx[:, 0:half_e]).T
-
-    @pl.when(is_last)
-    def _():
-        await_bytes(a_recv.at[pl.ds(0, group - 1)], psem_r.at[2])
-        a_lift[level] = jnp.sum(a_recv[...].astype(F32), axis=0).astype(BF16)
-        each_level(lambda to: push(a_lift.at[level], a_lift.at[level], 4, to))
-
-    @pl.when(jnp.logical_not(is_last))
-    def _():
-        await_bytes(a_recv.at[pl.ds(0, group - 1), narrow], psem_r.at[2])
-        a_lift[level, 0:share] = jnp.sum(a_recv[:, 0:share].astype(F32), axis=0).astype(BF16)
-        each_level(lambda to: push(a_lift.at[level, narrow], a_lift.at[level, narrow], 4, to))
 
     await_bytes(b_levels, psem_r.at[1])
     b_all[mine] = (jnp.sum(b_lift[...].astype(F32), axis=0) * factor).astype(BF16)

time: 38.1 us -> 38.1 us (level)
  no operation moved by 1% of the time
where the time goes in v7:
time: 38.1 us; the launch traced here: 37.9 us
  Pallas kernels  36.7 us (96%)
  between operations  1.29 us (3%)
    pallas_call x1, Pallas kernels, on_device(): pl.pallas_call(functools.partial(kernel, (peers, dps, plane, factor)), ou...  35.4 us
    pallas_call x1, Pallas kernels, on_device(): pl.pallas_call(deliver, out_shape=results, in_specs=[vmem] * 8, out_specs...  1.3 us

profile of v7, /device:TPU:1, one launch (start us, length us, event | category | flops | bytes accessed | tf_op | source)
XLA Modules:
  0.0 37.9 jit_solution(6236003395876221511)
XLA Ops:
  1.3 35.4 %shard_map.197 = (f32[512,128]{1,0:T(8,128)S(1)}, f32[2048,128]{1,0:T(8,128)S(1)}, f32[384,128]{1,0:T(8,128)S(1)}, f32[128,128]{1,0:T(8,128)S(1)}, f32[1,128]{1,...) custom-call(bf16[512,128]{1,0:T(8,128)(2,1)} %bitcast.12, ...), custom_call_target="tpu_custom_call" | custom-call | tf_op jit(solution)/shard_map/pallas_call | solution.py:456
  36.6 1.3 %shard_map.198 = (f32[512,128]{1,0:T(8,128)}, f32[2048,128]{1,0:T(8,128)}, f32[384,128]{1,0:T(8,128)}, f32[128,128]{1,0:T(8,128)}, f32[1,128]{1,0:T(1,128)}, /*i...) custom-call(f32[512,128]{1,0:T(8,128)S(1)} %get-tuple-element.24.refs_0_, ...), custom_call_target="tpu_custom_call" | custom-call | tf_op jit(solution)/shard_map/pallas_call | solution.py:480
